TPU v7x, 128 devices: a whole 4x4x4 slice. The times are simulated.
128 devices in a mesh: wide: 16 (over z, y_lo, core), narrow: 8 (over y_hi, x).
Axes of the slice: x: 4, y: 4 (y_hi: 2, y_lo: 2; y = y_hi * 2 + y_lo), z: 4, core: 2. Of those that a mesh axis runs over, the one named last changes fastest.
Arguments:
- queries: bfloat16 [1024, 8192], P('wide', 'narrow'), may hold values from -12 to 12
- tenant: int32 [1024], replicated, may hold values from 0 to 31
- tenant_node_slot: int32 [32], replicated, may hold values from 0 to 31, each once
- suffix_length: int32 [1024], P('wide'), may hold values from 1 to 256, 131072 in all
- system_prompt_cache: bfloat16 [32768, 8, 256], P('wide', 'narrow'), may hold values from -9 to 9
- instruction_node_cache: bfloat16 [32, 2048, 8, 256], P('narrow', 'wide'), may hold values from -9 to 9
- suffix_cache: bfloat16 [1024, 256, 8, 256], P('wide', None, 'narrow'), may hold values from -400 to 400
- output_projection_weight: bfloat16 [8192, 5120], P('narrow'), may hold values from -0.5 to 0.5
- adapter_down_weight: bfloat16 [8192, 512], P('narrow'), may hold values from -0.5 to 0.5
- adapter_up_weight: bfloat16 [512, 5120], P(None, 'narrow'), may hold values from -1.5 to 1.5
Outputs:
- projected: bfloat16 [1024, 5120], P('wide', 'narrow')
Inputs may be any that keep to these rules, and one draw needn't show every extreme that they name: `tenant_node_slot`: each of the 32 slots belongs to exactly one tenant. `suffix_length`: the longest suffix has exactly 256 positions.
All inputs are finite; a program needn't handle non-finite values. No bound on the sum of `suffix_length` on one device may be relied on, other than what follows from the above.
Results may differ from a plain program's by a relative error of at most 0.017.
Values may be sent and summed in bfloat16 or wider, within the bound.
No kernel may reach another device: no remote copies, remote signals or barrier semaphores. Data moves between devices by JAX's collectives and lax.ppermute only.
A program may use at most 320 MiB of HBM per device.

v0:
```python
import functools

import jax
import jax.numpy as jnp
from jax import lax
from jax.experimental import pallas as pl
from jax.experimental.pallas import tpu as pltpu
from jax.sharding import PartitionSpec as P

HEAD = 128
GROUP = 8
RANK = 16
F32 = jnp.float32
BF16 = jnp.bfloat16
SCALE2 = HEAD**-0.5 * 1.4426950408889634
FLOOR = -1e30
ROW_BLOCK = 256
KEY_BLOCK = 1024
VISIT_ROWS = 16
VISIT_UNROLL = 4
VMEM = 56 << 20


def _params():
    return pltpu.CompilerParams(
        vmem_limit_bytes=VMEM, dimension_semantics=("arbitrary",)
    )


def _lane(shape):
    return lax.broadcasted_iota(jnp.int32, shape, len(shape) - 1)


def _dot(a, b):
    return jnp.dot(a, b, preferred_element_type=F32)


def _system_kernel(q_ref, own_ref, sib_ref, o_ref, lse_ref, kt, ve):
    head = pl.program_id(0)
    n = own_ref.shape[0]

    @pl.when(head == 0)
    def _():
        for i, ref in enumerate((own_ref, sib_ref)):
            kt[:, i * n : (i + 1) * n] = ref[:, :HEAD].T
            ve[i * n : (i + 1) * n, :HEAD] = ref[:, HEAD:]
        ve[:, HEAD:] = jnp.ones((2 * n, HEAD), BF16)
        lse_ref[...] = jnp.zeros(lse_ref.shape, F32)

    rows = q_ref.shape[0]
    rb = min(ROW_BLOCK, rows)
    blocks = rows // rb
    lane = _lane((rb, HEAD))
    items = [(b, k) for b in range(blocks) for k in range(0, 2 * n, KEY_BLOCK)]

    def score(item):
        b, k = item
        return _dot(q_ref[b * rb : (b + 1) * rb, :], kt[:, k : k + KEY_BLOCK])

    top, total = [None] * blocks, [None] * blocks
    ahead = score(items[0])
    for i, (b, k) in enumerate(items):
        s = ahead
        if i + 1 < len(items):
            ahead = score(items[i + 1])
        high = jnp.max(s, axis=1, keepdims=True) * SCALE2
        if top[b] is not None:
            high = jnp.maximum(high, top[b])
        p = jnp.exp2(s * SCALE2 - high).astype(BF16)
        r = _dot(p, ve[k : k + KEY_BLOCK, :])
        if top[b] is None:
            total[b] = r
        else:
            total[b] = total[b] * jnp.exp2(top[b] - high) + r
        top[b] = high
    for b in range(blocks):
        l = total[b][:, HEAD:]
        at = slice(b * rb, (b + 1) * rb)
        o_ref[at, :] = total[b][:, :HEAD] / l
        lse = top[b] + jnp.log2(l)
        lse_ref[at, :] = jnp.where(lane == head, lse, lse_ref[at, :])


def _system(q, own, sib):
    rows, n = q.shape[0], own.shape[0]
    return pl.pallas_call(
        _system_kernel,
        grid=(GROUP,),
        in_specs=[
            pl.BlockSpec((rows, HEAD), lambda g: (0, g)),
            pl.BlockSpec((n, 2 * HEAD), lambda g: (0, 0)),
            pl.BlockSpec((n, 2 * HEAD), lambda g: (0, 0)),
        ],
        out_specs=[
            pl.BlockSpec((rows, HEAD), lambda g: (0, g)),
            pl.BlockSpec((rows, HEAD), lambda g: (0, 0)),
        ],
        out_shape=[
            jax.ShapeDtypeStruct((rows, GROUP * HEAD), F32),
            jax.ShapeDtypeStruct((rows, HEAD), F32),
        ],
        scratch_shapes=[
            pltpu.VMEM((HEAD, 2 * n), BF16),
            pltpu.VMEM((2 * n, 2 * HEAD), BF16),
        ],
        compiler_params=_params(),
        cost_estimate=pl.CostEstimate(
            flops=16 * rows * GROUP * n * HEAD,
            bytes_accessed=rows * 6 * GROUP * HEAD + 8 * n * HEAD,
            transcendentals=2 * rows * GROUP * n,
        ),
        name="system_attention",
    )(q, own, sib)


def _split3(x):
    hi = x.astype(BF16)
    rest = x - hi.astype(F32)
    mid = rest.astype(BF16)
    lo = (rest - mid.astype(F32)).astype(BF16)
    return hi.astype(F32), mid.astype(F32), lo.astype(F32)


def _pack3(x):
    lane = _lane(x.shape)
    hi, mid, lo = _split3(x)
    packed = jnp.where(lane < GROUP, hi, pltpu.roll(mid, GROUP, 1))
    packed = jnp.where(lane < 2 * GROUP, packed, pltpu.roll(lo, 2 * GROUP, 1))
    return jnp.where(lane < 3 * GROUP, packed, 0.0).astype(BF16)


def _unpack3(x):
    return x + (pltpu.roll(x, HEAD - GROUP, 1) + pltpu.roll(x, HEAD - 2 * GROUP, 1))


def _node_kernel(
    off_ref,
    slot_ref,
    q_ref,
    key_row_ref,
    key_col_ref,
    own_ref,
    sib_ref,
    o_sys_ref,
    lse_sys_ref,
    out_ref,
    qs,
    on,
    lse_n,
    visit_block,
    visit_tenant,
):
    rows = q_ref.shape[0]
    tenants = slot_ref.shape[0]
    vr = VISIT_ROWS

    def add_tenant(t, count):
        low, high = off_ref[t], off_ref[t + 1]
        first = low // vr
        last = jnp.where(high > low, (high + vr - 1) // vr, first)

        def add_block(b, c):
            visit_block[c] = b
            visit_tenant[c] = t
            return c + 1

        return lax.fori_loop(first, last, add_block, count)

    visits = lax.fori_loop(0, tenants, add_tenant, 0)
    for u in range(VISIT_UNROLL):
        visit_block[visits + u] = 0
        visit_tenant[visits + u] = tenants

    key_row, key_col = key_row_ref[...], key_col_ref[...]
    rank_row = jnp.sum((key_col < key_row).astype(jnp.int32), axis=0, keepdims=True)
    rank_col = jnp.sum((key_row < key_col).astype(jnp.int32), axis=1, keepdims=True)
    to_sorted = (
        lax.broadcasted_iota(jnp.int32, (rows, rows), 0) == rank_row
    ).astype(F32).astype(BF16)
    qs[...] = _dot(to_sorted, q_ref[...]).astype(BF16)

    lane = _lane((vr, HEAD))
    row_in_block = lax.broadcasted_iota(jnp.int32, (vr, HEAD), 0)

    def step(i, carry):
        blocks, spans, scores, slots = [], [], [], []
        for u in range(VISIT_UNROLL):
            v = i * VISIT_UNROLL + u
            b, t = visit_block[v], visit_tenant[v]
            slot = slot_ref[jnp.minimum(t, tenants - 1)]
            at = pl.ds(pl.multiple_of(b * vr, vr), vr)
            qb = jnp.concatenate(
                [qs[at, g * HEAD : (g + 1) * HEAD] for g in range(GROUP)], axis=0
            )
            dims = (((1,), (1,)), ((), ()))
            scores.append(
                [
                    lax.dot_general(
                        qb, ref[slot, :, :HEAD], dims, preferred_element_type=F32
                    )
                    for ref in (own_ref, sib_ref)
                ]
            )
            blocks.append(at)
            slots.append(slot)
            row = row_in_block + b * vr
            spans.append((row >= off_ref[t]) & (row < off_ref[t + 1]))
        tops, parts = [], []
        for s0, s1 in scores:
            high = jnp.max(jnp.maximum(s0, s1), axis=1, keepdims=True) * SCALE2
            p0 = jnp.exp2(s0 * SCALE2 - high)
            p1 = jnp.exp2(s1 * SCALE2 - high)
            tops.append(high)
            parts.append((p0, p1))
        results = []
        for (p0, p1), slot in zip(parts, slots):
            l = jnp.sum(p0 + p1, axis=1, keepdims=True)
            r = _dot(p0.astype(BF16), own_ref[slot, :, HEAD:]) + _dot(
                p1.astype(BF16), sib_ref[slot, :, HEAD:]
            )
            results.append((r, l))
        for at, inside, high, (r, l) in zip(blocks, spans, tops, results):
            o = r / l
            lse = high + jnp.log2(l)
            packed = jnp.zeros((vr, HEAD), F32)
            for g in range(GROUP):
                sub = slice(g * vr, (g + 1) * vr)
                cols = slice(g * HEAD, (g + 1) * HEAD)
                on[at, cols] = jnp.where(inside, o[sub, :], on[at, cols])
                packed = jnp.where(lane == g, lse[sub, :], packed)
            lse_n[at, :] = jnp.where(inside, packed, lse_n[at, :])
        return carry

    lax.fori_loop(0, (visits + VISIT_UNROLL - 1) // VISIT_UNROLL, step, 0)

    from_sorted = (
        lax.broadcasted_iota(jnp.int32, (rows, rows), 1) == rank_col
    ).astype(F32).astype(BF16)
    lse_node = _unpack3(_dot(from_sorted, _pack3(lse_n[...])))
    lse_sys = lse_sys_ref[...]
    top = jnp.maximum(lse_sys, lse_node)
    w_sys, w_node = jnp.exp2(lse_sys - top), jnp.exp2(lse_node - top)
    z = w_sys + w_node
    out_ref[:, GROUP * HEAD :] = _pack3(top + jnp.log2(z))
    w_sys, w_node = w_sys / z, w_node / z
    for g in range(GROUP):
        cols = slice(g * HEAD, (g + 1) * HEAD)
        o_node = _dot(from_sorted, on[:, cols].astype(BF16))
        out_ref[:, cols] = (
            w_sys[:, g : g + 1] * o_sys_ref[:, cols] + w_node[:, g : g + 1] * o_node
        ).astype(BF16)


def _node(off, slots, q, key, own, sib, o_sys, lse_sys):
    rows = q.shape[0]
    most = rows // VISIT_ROWS + slots.shape[0] + VISIT_UNROLL
    vmem = pl.BlockSpec(memory_space=pltpu.VMEM)
    return pl.pallas_call(
        _node_kernel,
        in_specs=[pl.BlockSpec(memory_space=pltpu.SMEM)] * 2 + [vmem] * 7,
        out_specs=vmem,
        out_shape=jax.ShapeDtypeStruct((rows, (GROUP + 1) * HEAD), BF16),
        scratch_shapes=[
            pltpu.VMEM((rows, GROUP * HEAD), BF16),
            pltpu.VMEM((rows, GROUP * HEAD), F32),
            pltpu.VMEM((rows, HEAD), F32),
            pltpu.SMEM((most,), jnp.int32),
            pltpu.SMEM((most,), jnp.int32),
        ],
        compiler_params=pltpu.CompilerParams(vmem_limit_bytes=VMEM),
        cost_estimate=pl.CostEstimate(
            flops=2 * 10**9, bytes_accessed=8 * 2**20, transcendentals=2**20
        ),
        name="node_attention",
    )(off, slots, q, key[None, :], key[:, None], own, sib, o_sys, lse_sys)


def _suffix_kernel(len_ref, q_ref, kv_ref, o_ref, lse_ref):
    rows, span = kv_ref.shape[0], kv_ref.shape[1]
    step = pl.program_id(0)
    position = _lane((GROUP, span))
    dims = (((1,), (1,)), ((), ()))
    scores = [
        lax.dot_general(
            q_ref[r], kv_ref[r, :, :HEAD], dims, preferred_element_type=F32
        )
        for r in range(rows)
    ]
    parts = []
    for r in range(rows):
        usable = position < len_ref[step * rows + r]
        s = jnp.where(usable, scores[r] * SCALE2, FLOOR)
        high = jnp.max(s, axis=1, keepdims=True)
        p = jnp.where(usable, jnp.exp2(s - high), 0.0)
        parts.append((p, high, jnp.sum(p, axis=1, keepdims=True)))
    for r in range(rows):
        p, high, l = parts[r]
        o_ref[r] = _dot(p.astype(BF16), kv_ref[r, :, HEAD:]) / l
        lse_ref[r] = jnp.broadcast_to(high + jnp.log2(l), (GROUP, HEAD))


def _suffix(lengths, q, kv):
    rows, span = kv.shape[0], kv.shape[1]
    block = 8
    shape = jax.ShapeDtypeStruct((rows, GROUP, HEAD), F32)
    spec = pl.BlockSpec((block, GROUP, HEAD), lambda i, n: (i, 0, 0))
    return pl.pallas_call(
        _suffix_kernel,
        grid_spec=pltpu.PrefetchScalarGridSpec(
            num_scalar_prefetch=1,
            grid=(rows // block,),
            in_specs=[
                spec,
                pl.BlockSpec((block, span, 2 * HEAD), lambda i, n: (i, 0, 0)),
            ],
            out_specs=[spec, spec],
        ),
        out_shape=[shape, shape],
        compiler_params=_params(),
        cost_estimate=pl.CostEstimate(
            flops=10**9, bytes_accessed=rows * span * 512, transcendentals=2**17
        ),
        name="suffix_attention",
    )(lengths, q.reshape(rows, GROUP, HEAD), kv)


def _project_kernel(
    tenant_ref, recv_ref, o_ref, lse_ref, w_ref, down_ref, out_ref, att, low
):
    parts, rows = recv_ref.shape[0], recv_ref.shape[1]

    @pl.when(pl.program_id(0) == 0)
    def _():
        lane = _lane((rows, HEAD))
        own = jnp.zeros((rows, HEAD), F32)
        for g in range(GROUP):
            own = jnp.where(lane == g, lse_ref[:, g, :], own)
        lses = [own] + [
            _unpack3(recv_ref[w, :, GROUP * HEAD :].astype(F32)) for w in range(parts)
        ]
        top = functools.reduce(jnp.maximum, lses)
        weights = [jnp.exp2(x - top) for x in lses]
        z = functools.reduce(jnp.add, weights)
        weights = [x / z for x in weights]
        for g in range(GROUP):
            cols = slice(g * HEAD, (g + 1) * HEAD)
            acc = weights[0][:, g : g + 1] * o_ref[:, g, :]
            for w in range(parts):
                acc += weights[1 + w][:, g : g + 1] * recv_ref[w, :, cols].astype(F32)
            att[:, cols] = acc.astype(BF16)
        reduced = _dot(att[...], down_ref[...])
        width = reduced.shape[1]
        mine = _lane((rows, width)) // RANK == tenant_ref[...]
        reduced = jnp.where(mine, reduced, 0.0)
        kept = reduced[:, :HEAD]
        for c in range(HEAD, width, HEAD):
            kept = kept + reduced[:, c : c + HEAD]
        low[...] = kept.astype(BF16)

    width = w_ref.shape[1]
    out_ref[0, :, :width] = _dot(att[...], w_ref[...]).astype(BF16)
    out_ref[0, :, width:] = low[...]


def _project(tenant, recv, o, lse, weight, down, parts):
    rows = recv.shape[1]
    depth, features = weight.shape
    width = features // parts

    def whole(shape):
        return pl.BlockSpec(shape, lambda d: (0,) * len(shape))

    return pl.pallas_call(
        _project_kernel,
        grid=(parts,),
        in_specs=[
            whole((rows, 1)),
            whole(recv.shape),
            whole(o.shape),
            whole(lse.shape),
            pl.BlockSpec((depth, width), lambda d: (0, d)),
            whole(down.shape),
        ],
        out_specs=pl.BlockSpec((1, rows, width + HEAD), lambda d: (d, 0, 0)),
        out_shape=jax.ShapeDtypeStruct((parts, rows, width + HEAD), BF16),
        scratch_shapes=[
            pltpu.VMEM((rows, GROUP * HEAD), BF16),
            pltpu.VMEM((rows, HEAD), BF16),
        ],
        compiler_params=_params(),
        cost_estimate=pl.CostEstimate(
            flops=2 * rows * depth * features,
            bytes_accessed=2 * depth * features,
            transcendentals=0,
        ),
        name="project",
    )(tenant, recv, o, lse, weight, down)


def _finish_kernel(tenant_ref, recv_ref, up_ref, out_ref):
    parts, rows = recv_ref.shape[0], recv_ref.shape[1]
    width = out_ref.shape[1]
    total = recv_ref[0].astype(F32)
    for w in range(1, parts):
        total += recv_ref[w].astype(F32)
    depth = up_ref.shape[0]
    low = jnp.concatenate([total[:, width:]] * (depth // HEAD), axis=1)
    mine = _lane((rows, depth)) // RANK == tenant_ref[...]
    chosen = jnp.where(mine, low, 0.0).astype(BF16)
    out_ref[...] = (total[:, :width] + _dot(chosen, up_ref[...])).astype(BF16)


def _finish(tenant, recv, up):
    vmem = pl.BlockSpec(memory_space=pltpu.VMEM)
    return pl.pallas_call(
        _finish_kernel,
        in_specs=[vmem] * 3,
        out_specs=vmem,
        out_shape=jax.ShapeDtypeStruct((recv.shape[1], up.shape[1]), BF16),
        compiler_params=pltpu.CompilerParams(vmem_limit_bytes=VMEM),
        name="finish",
    )(tenant, recv, up)


def per_device(
    queries,
    tenant,
    tenant_node_slot,
    suffix_length,
    system_prompt_cache,
    instruction_node_cache,
    suffix_cache,
    output_projection_weight,
    adapter_down_weight,
    adapter_up_weight,
):
    rows, width = queries.shape
    n_wide = lax.axis_size("wide")
    n_narrow = lax.axis_size("narrow")
    chips = n_wide // 2
    position = lax.axis_index("wide")
    core = position % 2
    same_core = [[2 * j + c for j in range(chips)] for c in range(2)]
    sibling = [(i, i ^ 1) for i in range(n_wide)]
    n_slots = tenant_node_slot.shape[0]
    span = instruction_node_cache.shape[1]

    q = lax.all_to_all(
        jnp.broadcast_to(queries[None], (chips, rows, width)),
        "wide",
        0,
        0,
        axis_index_groups=same_core,
        tiled=True,
    ).reshape(chips * rows, width)

    own = system_prompt_cache.reshape(-1, 2 * HEAD)
    sib = lax.ppermute(own, "wide", sibling)

    by_head = jnp.transpose(instruction_node_cache, (2, 0, 1, 3))
    q, by_head = lax.optimization_barrier((q, by_head))
    nodes = lax.all_to_all(by_head, "narrow", 0, 0, tiled=True)
    nodes = nodes.reshape(n_slots, span, 2 * HEAD)
    nodes_sib = lax.ppermute(nodes, "wide", sibling)

    by_core = tenant.reshape(chips, 2, rows)
    mine = jnp.where(core == 0, by_core[:, 0], by_core[:, 1]).reshape(-1)
    key = mine * (chips * rows) + jnp.arange(chips * rows, dtype=jnp.int32)
    bounds = jnp.arange(n_slots + 2, dtype=jnp.int32)
    off = jnp.sum((mine[None, :] < bounds[:, None]).astype(jnp.int32), axis=1)

    o_suf, lse_suf = _suffix(
        suffix_length, queries, suffix_cache.reshape(rows, -1, 2 * HEAD)
    )
    o_sys, lse_sys = _system(q, own, sib)
    sent = _node(off, tenant_node_slot, q, key, nodes, nodes_sib, o_sys, lse_sys)
    recv = lax.all_to_all(
        sent.reshape(chips, rows, -1),
        "wide",
        0,
        0,
        axis_index_groups=same_core,
        tiled=True,
    )
    my_tenant = lax.dynamic_slice_in_dim(tenant, position * rows, rows, 0)[:, None]
    parts = _project(
        my_tenant,
        recv,
        o_suf,
        lse_suf,
        output_projection_weight,
        adapter_down_weight,
        n_narrow,
    )
    parts = lax.all_to_all(parts, "narrow", 0, 0, tiled=True)
    return _finish(my_tenant, parts, adapter_up_weight)


def solution(mesh):
    return jax.shard_map(
        per_device,
        mesh=mesh,
        in_specs=(
            P("wide", "narrow"),
            P(),
            P(),
            P("wide"),
            P("wide", "narrow", None),
            P("narrow", "wide", None, None),
            P("wide", None, "narrow", None),
            P("narrow", None),
            P("narrow", None),
            P(None, "narrow"),
        ),
        out_specs=P("wide", "narrow"),
        check_vma=False,
    )
```

profile of v0, /device:TPU:0, one launch (start us, length us, event | category | flops | bytes accessed | tf_op | source)
XLA Modules:
  0.0 162.0 jit_solution(17079563619951461949)
XLA Ops:
  0.0 2.2 %broadcast_in_dim.5 = bf16[8,64,1024]{2,1,0:T(8,128)(2,1)} broadcast(bf16[64,1024]{1,0:T(8,128)(2,1)} %param.10), dimensions={1,2} | broadcast | bytes 1179648 | tf_op jit(solution)/shard_map/broadcast_in_dim | solution.py:449
  2.2 6.4 %all-to-all-start = ((bf16[8,64,1024]{2,1,0:T(8,128)(2,1)}), bf16[8,64,1024]{2,1,0:T(8,128)(2,1)S(1)}, u32[]{:S(2)}, u32[]{:S(2)}) async-start(bf16[8,64,1024]{2,1,0:T(8,128)(2,1)} %broadcast_in_dim.5), calls=%async_computation | async-start | bytes 2097152 | tf_op jit(solution)/shard_map/all_to_all | solution.py:448
  8.6 1.8 %copy.28 = bf16[4,128,8,256]{3,1,0,2:T(8,128)(2,1)} copy(bf16[4,128,8,256]{3,2,1,0:T(8,128)(2,1)S(1)} %copy-done.3) | data formatting | bytes 4194304 | tf_op args[5]
  10.4 13.9 %all-to-all-done = bf16[8,64,1024]{2,1,0:T(8,128)(2,1)S(1)} async-done(((bf16[8,64,1024]{2,1,0:T(8,128)(2,1)}), bf16[8,64,1024]{2,1,0:T(8,128)(2,1)S(1)}, u32[]{:S(2)}, u32[]{:S(2)}) %all-to-all-start) | async-done | bytes 1048608 | tf_op jit(solution)/shard_map/all_to_all | solution.py:448
  24.3 1.0 copy-done.2
  25.3 6.6 %all-to-all-start.1 = ((bf16[8,4,128,256]{3,2,1,0:T(8,128)(2,1)}), bf16[8,4,128,256]{3,2,1,0:T(8,128)(2,1)S(1)}, u32[]{:S(2)}, u32[]{:S(2)}) async-start(bf16[8,4,128,256]{3,2,1,0:T(8,128)(2,1)} %bitcast.12), calls=%async_computation.1 | async-start | bytes 4194304 | tf_op jit(solution)/shard_map/all_to_all | solution.py:462
  32.1 0.5 broadcast.52
  32.6 0.7 fusion
  33.3 25.6 %all-to-all-done.1 = bf16[8,4,128,256]{3,2,1,0:T(8,128)(2,1)S(1)} async-done(((bf16[8,4,128,256]{3,2,1,0:T(8,128)(2,1)}), bf16[8,4,128,256]{3,2,1,0:T(8,128)(2,1)S(1)}, u32[]{:S(2)}, u32[]{:S(2)}) %all-to-all-start.1) | async-done | bytes 2097184 | tf_op jit(solution)/shard_map/all_to_all | solution.py:462
  58.9 0.7 convert_reduce_fusion.off_ref
  59.9 0.6 iota_add_fusion.1.key_row_ref
  60.5 0.7 iota_add_fusion.key_col_ref
  61.3 1.0 copy-done.6
  62.3 25.6 %system_attention.1 = (f32[512,1024]{1,0:T(8,128)}, f32[512,128]{1,0:T(8,128)}) custom-call(bf16[512,1024]{1,0:T(8,128)(2,1)} %bitcast.17, bf16[2048,256]{1,0:T(8,128)(2,1)} %bitcast.23, bf16[2048,256]{1,0:T(8,128)(2,1)} %copy-done.6), custom_call_target="tpu_custom_call" | custom-call | flops 17179869184 | bytes 5242880 | tf_op jit(solution)/shard_map/system_attention/pallas_call | solution.py:86
  87.9 16.5 %node_attention.1 = bf16[512,1152]{1,0:T(8,128)(2,1)} custom-call(s32[34]{0:T(128)} %convert_reduce_fusion.off_ref, s32[32]{0:T(128)} %slot_ref.1, bf16[512,1024]{1,0:T(8,128)(2,1)} %bitcast.18, s32[1,512]{1,0:T(1,128)} %iota_add_fusion.1.key_row_ref, s32[512,1]{1,0:T(8,128)} %iota_add_fusion.key_col_ref, bf16[32,128,256]{2,1,0:T(8,128)(2,1)} %bitcast.15, ...), custom_call_target="tpu_custom_call" | custom-call | flops 2000000000 | bytes 8388608 | tf_op jit(solution)/shard_map/node_attention/pallas_call | solution.py:258
  104.4 3.9 %all-to-all-start.2 = ((bf16[8,64,1152]{2,1,0:T(8,128)(2,1)}), bf16[8,64,1152]{2,1,0:T(8,128)(2,1)S(1)}, u32[]{:S(2)}, u32[]{:S(2)}) async-start(bf16[8,64,1152]{2,1,0:T(8,128)(2,1)} %bitcast.16), calls=%async_computation.2 | async-start | bytes 2359296 | tf_op jit(solution)/shard_map/all_to_all | solution.py:477
  108.4 0.7 copy.25.tenant_ref
  109.1 0.7 copy.26
  109.8 8.9 %suffix_attention.1 = (f32[64,8,128]{2,1,0:T(8,128)}, f32[64,8,128]{2,1,0:T(8,128)}) custom-call(s32[64]{0:T(128)} %len_ref.1, bf16[64,8,128]{2,1,0:T(8,128)(2,1)} %bitcast.19, bf16[64,256,256]{2,1,0:T(8,128)(2,1)} %bitcast.13), custom_call_target="tpu_custom_call" | custom-call | flops 1000000000 | bytes 8388608 | tf_op jit(solution)/shard_map/suffix_attention/pallas_call | solution.py:307
  118.7 7.9 %all-to-all-done.2.recv_ref = bf16[8,64,1152]{2,1,0:T(8,128)(2,1)S(1)} async-done(((bf16[8,64,1152]{2,1,0:T(8,128)(2,1)}), bf16[8,64,1152]{2,1,0:T(8,128)(2,1)S(1)}, u32[]{:S(2)}, u32[]{:S(2)}) %all-to-all-start.2) | async-done | bytes 1179680 | tf_op jit(solution)/shard_map/all_to_all | solution.py:477
  126.6 1.0 copy-done.1
  127.6 10.3 %project.1 = bf16[8,64,768]{2,1,0:T(8,128)(2,1)} custom-call(s32[64,1]{1,0:T(8,128)} %copy.25.tenant_ref, bf16[8,64,1152]{2,1,0:T(8,128)(2,1)} %copy-done.1, f32[64,8,128]{2,1,0:T(8,128)} %get-tuple-element.15.o_ref, f32[64,8,128]{2,1,0:T(8,128)} %get-tuple-element.16.lse_ref, bf16[1024,5120]{1,0:T(8,128)(2,1)} %w_ref.1, bf16[1024,512]{1,0:T(8,128)(2,1)} %down_ref.1), custom_call_target="tpu_custom_call" | custom-call | flops 671088640 | bytes 10485760 | tf_op jit(solution)/shard_map/project/pallas_call | solution.py:373
  138.0 21.8 %all_to_all.20.recv_ref = bf16[8,64,768]{2,1,0:T(8,128)(2,1)} all-to-all(bf16[8,64,768]{2,1,0:T(8,128)(2,1)} %project.1), channel_id=1, replica_groups=mesh['wide'=16,'narrow'=8] {'narrow'}, dimensions={0} | all-to-all | bytes 1572864 | tf_op jit(solution)/shard_map/all_to_all | solution.py:495
  159.7 2.3 %finish.1 = bf16[64,640]{1,0:T(8,128)(2,1)} custom-call(s32[64,1]{1,0:T(8,128)} %copy.25.tenant_ref, bf16[8,64,768]{2,1,0:T(8,128)(2,1)} %all_to_all.20.recv_ref, bf16[512,640]{1,0:T(8,128)(2,1)} %up_ref.1), custom_call_target="tpu_custom_call" | custom-call | tf_op jit(solution)/shard_map/finish/pallas_call | solution.py:415
  (21 shorter events, 0.5 us)
Async XLA Ops:
  0.0 8.6 %copy-start.3 = (bf16[4,128,8,256]{3,2,1,0:T(8,128)(2,1)S(1)}, bf16[4,128,8,256]{3,2,1,0:T(8,128)(2,1)}, u32[]{:S(2)}) copy-start(bf16[4,128,8,256]{3,2,1,0:T(8,128)(2,1)} %param.15) | copy-start | bytes 6291460
  2.2 22.1 %all-to-all-start = ((bf16[8,64,1024]{2,1,0:T(8,128)(2,1)}), bf16[8,64,1024]{2,1,0:T(8,128)(2,1)S(1)}, u32[]{:S(2)}, u32[]{:S(2)}) async-start(bf16[8,64,1024]{2,1,0:T(8,128)(2,1)} %broadcast_in_dim.5), calls=%async_computation | async-start | bytes 2097152 | tf_op jit(solution)/shard_map/all_to_all | solution.py:448
  24.3 1.0 copy-start.2
  24.3 7.7 %copy-start.5 = (s32[1024]{0:T(1024)S(1)}, s32[1024]{0:T(1024)}, u32[]{:S(2)}) copy-start(s32[1024]{0:T(1024)} %param.11) | copy-start | bytes 12292
  25.3 33.6 %all-to-all-start.1 = ((bf16[8,4,128,256]{3,2,1,0:T(8,128)(2,1)}), bf16[8,4,128,256]{3,2,1,0:T(8,128)(2,1)S(1)}, u32[]{:S(2)}, u32[]{:S(2)}) async-start(bf16[8,4,128,256]{3,2,1,0:T(8,128)(2,1)} %bitcast.12), calls=%async_computation.1 | async-start | bytes 4194304 | tf_op jit(solution)/shard_map/all_to_all | solution.py:462
  32.0 29.3 %collective-permute-start.1 = (bf16[2048,256]{1,0:T(8,128)(2,1)}, bf16[2048,256]{1,0:T(8,128)(2,1)S(1)}, u32[]{:S(2)}, u32[]{:S(2)}) collective-permute-start(bf16[2048,256]{1,0:T(8,128)(2,1)} %bitcast.22), channel_id=1, source_target_pairs={{0,8},{8,0},{16,24},{24,16},{32,40},{40,32},{48,56},{56,48},{64,72... | collective-permute-start | bytes 3145736 | tf_op jit(solution)/shard_map/ppermute | solution.py:458
  58.9 29.0 %copy-start = (bf16[8,4,128,256]{3,2,1,0:T(8,128)(2,1)}, bf16[8,4,128,256]{3,2,1,0:T(8,128)(2,1)S(1)}, u32[]{:S(2)}) copy-start(bf16[8,4,128,256]{3,2,1,0:T(8,128)(2,1)S(1)} %all-to-all-done.1) | copy-start | bytes 6291460
  58.9 29.0 %collective-permute-start = (bf16[32,128,256]{2,1,0:T(8,128)(2,1)S(1)}, bf16[32,128,256]{2,1,0:T(8,128)(2,1)}, u32[]{:S(2)}, u32[]{:S(2)}) collective-permute-start(bf16[32,128,256]{2,1,0:T(8,128)(2,1)S(1)} %bitcast.14), channel_id=1, source_target_pairs={{0,8},{8,0},{16,24},{24,16},{32,40},{40,32},{48,56},{56,48},{64,72... | collective-permute-start | bytes 6291464 | tf_op jit(solution)/shard_map/ppermute | solution.py:464
  61.3 1.0 copy-start.6
  104.4 4.7 %copy-start.4 = (bf16[64,1024]{1,0:T(8,128)(2,1)S(1)}, bf16[64,1024]{1,0:T(8,128)(2,1)}, u32[]{:S(2)}) copy-start(bf16[64,1024]{1,0:T(8,128)(2,1)} %param.10) | copy-start | bytes 393220
  104.4 22.2 %all-to-all-start.2 = ((bf16[8,64,1152]{2,1,0:T(8,128)(2,1)}), bf16[8,64,1152]{2,1,0:T(8,128)(2,1)S(1)}, u32[]{:S(2)}, u32[]{:S(2)}) async-start(bf16[8,64,1152]{2,1,0:T(8,128)(2,1)} %bitcast.16), calls=%async_computation.2 | async-start | bytes 2359296 | tf_op jit(solution)/shard_map/all_to_all | solution.py:477
  126.6 1.0 copy-start.1
where the time goes:
time: 163 us; the launch traced here: 162 us
  Pallas kernels  63.6 us (39%)
  waiting for transfers between devices  47.3 us (29%)
  blocking collectives  21.8 us (13%)
  starting transfers between devices  17 us (10%)
  local copies, waits for them, and re-layouts  9.42 us (6%)
  other arithmetic  2.75 us (2%)
    pallas_call x1, Pallas kernels, _system(): pl.pallas_call(_system_kernel, grid=(GROUP,), in_specs=[pl.BlockSpec((row...  25.6 us
    all_to_all x1, waiting for transfers between devices, per_device(): nodes = lax.all_to_all(by_head, 'narrow', 0, 0, tiled=True)  25.6 us
    all_to_all x1, blocking collectives, per_device(): parts = lax.all_to_all(parts, 'narrow', 0, 0, tiled=True)  21.8 us
    pallas_call x1, Pallas kernels, _node(): pl.pallas_call(_node_kernel, in_specs=[pl.BlockSpec(memory_space=pltpu.SM...  16.5 us
    all_to_all x1, waiting for transfers between devices, per_device(): lax.all_to_all(jnp.broadcast_to(queries[None], (chips, rows, width)), 'wi...  13.9 us
    pallas_call x1, Pallas kernels, _project(): pl.pallas_call(_project_kernel, grid=(parts,), in_specs=[whole((rows, 1))...  10.3 us
    pallas_call x1, Pallas kernels, _suffix(): pl.pallas_call(_suffix_kernel, grid_spec=pltpu.PrefetchScalarGridSpec(num...  8.94 us
    all_to_all x1, waiting for transfers between devices, per_device(): lax.all_to_all(sent.reshape(chips, rows, -1), 'wide', 0, 0, axis_index_gr...  7.89 us
  transfers between devices with their start and end apart: 5, of which 3 were waited for; matrix products, arithmetic and copies ran while one was open for 4% of the time, Pallas kernels for 21%

commit v1 on v0

v1 whole, which is shorter than its diff:
```python
import functools

import jax
import jax.numpy as jnp
from jax import lax
from jax.experimental import pallas as pl
from jax.experimental.pallas import tpu as pltpu
from jax.sharding import PartitionSpec as P

HEAD = 128
GROUP = 8
RANK = 16
F32 = jnp.float32
BF16 = jnp.bfloat16
SCALE2 = HEAD**-0.5 * 1.4426950408889634
FLOOR = -1e30
KEY_BLOCK = 2048
HEADS_AT_ONCE = 2
VISIT_ROWS = 16
VISIT_UNROLL = 8


def _params(mib, grid=True):
    return pltpu.CompilerParams(
        vmem_limit_bytes=mib << 20,
        dimension_semantics=("arbitrary",) if grid else None,
    )


def _in_hbm(x):
    return pltpu.with_memory_space_constraint(x, pltpu.HBM)


def _lane(shape):
    return lax.broadcasted_iota(jnp.int32, shape, len(shape) - 1)


def _dot(a, b):
    return jnp.dot(a, b, preferred_element_type=F32)


def _keys_kernel(own_ref, sib_ref, kt_ref, ve_ref):
    n = own_ref.shape[0]
    for i, ref in enumerate((own_ref, sib_ref)):
        at = slice(i * n, (i + 1) * n)
        kt_ref[:, at] = ref[:, :HEAD].T
        ve_ref[at, :HEAD] = ref[:, HEAD:]
        ve_ref[at, HEAD:] = jnp.ones((n, HEAD), BF16)


def _keys(own, sib):
    n = 2 * own.shape[0]
    vmem = pl.BlockSpec(memory_space=pltpu.VMEM)
    return pl.pallas_call(
        _keys_kernel,
        in_specs=[vmem] * 2,
        out_specs=[vmem] * 2,
        out_shape=[
            jax.ShapeDtypeStruct((HEAD, n), BF16),
            jax.ShapeDtypeStruct((n, 2 * HEAD), BF16),
        ],
        compiler_params=_params(16, False),
        cost_estimate=pl.CostEstimate(
            flops=0, bytes_accessed=10 * n * HEAD, transcendentals=0
        ),
        name="keys",
    )(own, sib)


def _system_kernel(count, *refs):
    q_refs, (kt, ve) = refs[:count], refs[count : count + 2]
    o_refs, lse_refs = refs[count + 2 : 2 * count + 2], refs[2 * count + 2 :]
    step = pl.program_id(0)
    rows, keys = q_refs[0].shape[0], kt.shape[1]
    lane = _lane((rows, HEAD))
    items = [
        (h, b, k)
        for h in range(HEADS_AT_ONCE)
        for b in range(count)
        for k in range(0, keys, KEY_BLOCK)
    ]

    def score(item):
        h, b, k = item
        q = q_refs[b][:, h * HEAD : (h + 1) * HEAD]
        return _dot(q, kt[:, k : k + KEY_BLOCK])

    top, total = {}, {}
    ahead = score(items[0])
    for i, (h, b, k) in enumerate(items):
        s = ahead
        if i + 1 < len(items):
            ahead = score(items[i + 1])
        high = jnp.max(s, axis=1, keepdims=True) * SCALE2
        if (h, b) in top:
            high = jnp.maximum(high, top[h, b])
        p = jnp.exp2(s * SCALE2 - high).astype(BF16)
        r = _dot(p, ve[k : k + KEY_BLOCK, :])
        if (h, b) in top:
            r = total[h, b] * jnp.exp2(top[h, b] - high) + r
        top[h, b], total[h, b] = high, r
    for b in range(count):
        packed = jnp.where(step == 0, 0.0, lse_refs[b][...])
        for h in range(HEADS_AT_ONCE):
            l = total[h, b][:, HEAD:]
            o_refs[b][:, h * HEAD : (h + 1) * HEAD] = total[h, b][:, :HEAD] / l
            lse = top[h, b] + jnp.log2(l)
            packed = jnp.where(lane == step * HEADS_AT_ONCE + h, lse, packed)
        lse_refs[b][...] = packed


def _system(qs, kt, ve):
    count, rows, keys = len(qs), qs[0].shape[0], ve.shape[0]
    heads = pl.BlockSpec((rows, HEADS_AT_ONCE * HEAD), lambda g: (0, g))
    fixed = pl.BlockSpec((rows, HEAD), lambda g: (0, 0))
    outs = pl.pallas_call(
        functools.partial(_system_kernel, count),
        grid=(GROUP // HEADS_AT_ONCE,),
        in_specs=[heads] * count
        + [
            pl.BlockSpec(kt.shape, lambda g: (0, 0)),
            pl.BlockSpec(ve.shape, lambda g: (0, 0)),
        ],
        out_specs=[heads] * count + [fixed] * count,
        out_shape=[pltpu.HBM((rows, GROUP * HEAD), F32)] * count
        + [pltpu.HBM((rows, HEAD), F32)] * count,
        compiler_params=_params(32),
        cost_estimate=pl.CostEstimate(
            flops=6 * count * rows * GROUP * keys * HEAD,
            bytes_accessed=count * rows * 6 * GROUP * HEAD + 6 * keys * HEAD,
            transcendentals=count * rows * GROUP * keys,
        ),
        name="system_attention",
    )(*qs, kt, ve)
    return list(outs[:count]), list(outs[count:])


def _split3(x):
    hi = x.astype(BF16)
    rest = x - hi.astype(F32)
    mid = rest.astype(BF16)
    lo = (rest - mid.astype(F32)).astype(BF16)
    return hi.astype(F32), mid.astype(F32), lo.astype(F32)


def _pack3(x):
    lane = _lane(x.shape)
    hi, mid, lo = _split3(x)
    packed = jnp.where(lane < GROUP, hi, pltpu.roll(mid, GROUP, 1))
    packed = jnp.where(lane < 2 * GROUP, packed, pltpu.roll(lo, 2 * GROUP, 1))
    return jnp.where(lane < 3 * GROUP, packed, 0.0).astype(BF16)


def _unpack3(x):
    return x + (pltpu.roll(x, HEAD - GROUP, 1) + pltpu.roll(x, HEAD - 2 * GROUP, 1))


def _plan_kernel(slot_ref, row_ref, col_ref, *refs):
    q_refs, (qs_ref, back_ref, table_ref) = refs[:-3], refs[-3:]
    rows = qs_ref.shape[0]
    piece = q_refs[0].shape[0]
    tenants = slot_ref.shape[0]
    width = table_ref.shape[1]
    t_row, t_col = row_ref[...], col_ref[...]

    def iota(shape, dim):
        return lax.broadcasted_iota(jnp.int32, shape, dim)

    def count(where, axis):
        return jnp.sum(where.astype(jnp.int32), axis=axis, keepdims=True)

    key_row = t_row * rows + iota((1, rows), 1)
    key_col = t_col * rows + iota((rows, 1), 0)
    rank_row = count(key_col < key_row, 0)
    rank_col = count(key_row < key_col, 1)
    to_sorted = (iota((rows, rows), 0) == rank_row).astype(F32).astype(BF16)
    back_ref[...] = (iota((rows, rows), 1) == rank_col).astype(F32).astype(BF16)
    qs_ref[...] = sum(
        _dot(to_sorted[:, i * piece : (i + 1) * piece], ref[...])
        for i, ref in enumerate(q_refs)
    ).astype(BF16)

    def visits_of(low, high):
        first = low // VISIT_ROWS
        last = (high + VISIT_ROWS - 1) // VISIT_ROWS
        return first, jnp.where(high > low, last - first, 0)

    lane = iota((1, width), 1)
    _, n_row = visits_of(count(t_col < lane, 0), count(t_col < lane + 1, 0))
    t = iota((tenants, 1), 0)
    low, high = count(t_row < t, 1), count(t_row < t + 1, 1)
    first, n = visits_of(low, high)
    start = jnp.sum(jnp.where(lane < t, n_row, 0), axis=1, keepdims=True)
    here = (lane >= start) & (lane < start + n)

    def pick(column):
        return jnp.sum(jnp.where(here, column, 0), axis=0, keepdims=True)

    table_ref[...] = jnp.concatenate(
        [
            pick(first - start + lane),
            pick(slot_ref[...]),
            pick(low),
            pick(high),
            jnp.broadcast_to(jnp.sum(n, axis=0, keepdims=True), (1, width)),
        ]
        + [jnp.zeros((1, width), jnp.int32)] * 3,
        axis=0,
    )


def _plan(slots, mine, qs):
    rows, width = mine.shape[0], qs[0].shape[1]
    vmem = pl.BlockSpec(memory_space=pltpu.VMEM)
    return pl.pallas_call(
        _plan_kernel,
        in_specs=[vmem] * (3 + len(qs)),
        out_specs=[vmem] * 3,
        out_shape=[
            jax.ShapeDtypeStruct((rows, width), BF16),
            jax.ShapeDtypeStruct((rows, rows), BF16),
            jax.ShapeDtypeStruct((8, HEAD), jnp.int32),
        ],
        compiler_params=_params(16, False),
        cost_estimate=pl.CostEstimate(
            flops=2 * rows * rows * width,
            bytes_accessed=6 * rows * width,
            transcendentals=0,
        ),
        name="plan",
    )(slots[:, None], mine[None, :], mine[:, None], *qs)


def _node_kernel(count, table, order, qs, back_ref, own_ref, sib_ref, *refs):
    o_hbm, lse_hbm = refs[:count], refs[count : 2 * count]
    out_ref, on, lse_n, o_buf, lse_buf, sems = refs[2 * count :]
    fetches = [
        pltpu.make_async_copy(src, dst, sems.at[i])
        for i, (src, dst) in enumerate(
            [(o_hbm[i], o_buf.at[i]) for i in range(count)]
            + [(lse_hbm[i], lse_buf.at[i]) for i in range(count)]
        )
    ]
    for fetch in fetches:
        fetch.start()
    vr = VISIT_ROWS
    lane = _lane((vr, HEAD))
    row_in_block = lax.broadcasted_iota(jnp.int32, (vr, HEAD), 0)
    dims = (((1,), (1,)), ((), ()))

    def step(i, carry):
        blocks, spans, scores, slots = [], [], [], []
        for u in range(VISIT_UNROLL):
            v = i * VISIT_UNROLL + u
            at = pl.ds(pl.multiple_of(table[0, v] * vr, vr), vr)
            slot = table[1, v]
            qb = jnp.concatenate(
                [qs[at, g * HEAD : (g + 1) * HEAD] for g in range(GROUP)], axis=0
            )
            scores.append(
                [
                    lax.dot_general(
                        qb, ref[slot, :, :HEAD], dims, preferred_element_type=F32
                    )
                    for ref in (own_ref, sib_ref)
                ]
            )
            blocks.append(at)
            slots.append(slot)
            row = row_in_block + table[0, v] * vr
            spans.append((row >= table[2, v]) & (row < table[3, v]))
        tops, parts = [], []
        for s0, s1 in scores:
            high = jnp.max(jnp.maximum(s0, s1), axis=1, keepdims=True) * SCALE2
            p0 = jnp.exp2(s0 * SCALE2 - high)
            p1 = jnp.exp2(s1 * SCALE2 - high)
            tops.append(high)
            parts.append((p0, p1))
        results = []
        for (p0, p1), slot in zip(parts, slots):
            l = jnp.sum(p0 + p1, axis=1, keepdims=True)
            r = _dot(p0.astype(BF16), own_ref[slot, :, HEAD:]) + _dot(
                p1.astype(BF16), sib_ref[slot, :, HEAD:]
            )
            results.append((r, l))
        for at, inside, high, (r, l) in zip(blocks, spans, tops, results):
            o = r / l
            lse = high + jnp.log2(l)
            packed = jnp.zeros((vr, HEAD), F32)
            for g in range(GROUP):
                sub = slice(g * vr, (g + 1) * vr)
                cols = slice(g * HEAD, (g + 1) * HEAD)
                on[at, cols] = jnp.where(inside, o[sub, :], on[at, cols].astype(F32)).astype(
                    BF16
                )
                packed = jnp.where(lane == g, lse[sub, :], packed)
            lse_n[at, :] = jnp.where(inside, packed, lse_n[at, :])
        return carry

    lax.fori_loop(0, (table[4, 0] + VISIT_UNROLL - 1) // VISIT_UNROLL, step, 0)

    for fetch in fetches:
        fetch.wait()
    packed_lse = _pack3(lse_n[...])
    piece = o_buf.shape[1]
    for i in range(count):
        back = back_ref[i * piece : (i + 1) * piece, :]
        to = pl.ds(pl.multiple_of(order[i] * piece, piece), piece)
        lse_node = _unpack3(_dot(back, packed_lse))
        lse_sys = lse_buf[i]
        top = jnp.maximum(lse_sys, lse_node)
        w_sys, w_node = jnp.exp2(lse_sys - top), jnp.exp2(lse_node - top)
        z = w_sys + w_node
        out_ref[to, GROUP * HEAD :] = _pack3(top + jnp.log2(z))
        w_sys, w_node = w_sys / z, w_node / z
        for g in range(GROUP):
            cols = slice(g * HEAD, (g + 1) * HEAD)
            o_node = _dot(back, on[:, cols])
            out_ref[to, cols] = (
                w_sys[:, g : g + 1] * o_buf[i, :, cols]
                + w_node[:, g : g + 1] * o_node
            ).astype(BF16)


def _node(table, order, qs, back, own, sib, o_sys, lse_sys):
    rows, count = qs.shape[0], len(o_sys)
    smem = pl.BlockSpec(memory_space=pltpu.SMEM)
    hbm = pl.BlockSpec(memory_space=pltpu.HBM)
    piece = o_sys[0].shape[0]
    vmem = pl.BlockSpec(memory_space=pltpu.VMEM)
    return pl.pallas_call(
        functools.partial(_node_kernel, count),
        in_specs=[smem] * 2 + [vmem] * 4 + [hbm] * (2 * count),
        out_specs=vmem,
        out_shape=jax.ShapeDtypeStruct((rows, (GROUP + 1) * HEAD), BF16),
        scratch_shapes=[
            pltpu.VMEM((rows, GROUP * HEAD), BF16),
            pltpu.VMEM((rows, HEAD), F32),
            pltpu.VMEM((count, piece, GROUP * HEAD), F32),
            pltpu.VMEM((count, piece, HEAD), F32),
            pltpu.SemaphoreType.DMA((2 * count,)),
        ],
        compiler_params=_params(24, False),
        cost_estimate=pl.CostEstimate(
            flops=2 * 10**9, bytes_accessed=8 * 2**20, transcendentals=2**20
        ),
        name="node_attention",
    )(table, order, qs, back, own, sib, *map(_in_hbm, [*o_sys, *lse_sys]))


def _suffix_kernel(len_ref, q_ref, kv_hbm, o_ref, lse_ref, kv_ref, sems):
    rows, span = kv_ref.shape[0], kv_ref.shape[1]
    block = rows // sems.shape[0]
    fetches = [
        pltpu.make_async_copy(
            kv_hbm.at[pl.ds(i * block, block)],
            kv_ref.at[pl.ds(i * block, block)],
            sems.at[i],
        )
        for i in range(sems.shape[0])
    ]
    for fetch in fetches:
        fetch.start()
    position = _lane((GROUP, span))
    dims = (((1,), (1,)), ((), ()))
    for i, fetch in enumerate(fetches):
        fetch.wait()
        here = range(i * block, (i + 1) * block)
        scores = [
            lax.dot_general(
                q_ref[r], kv_ref[r, :, :HEAD], dims, preferred_element_type=F32
            )
            for r in here
        ]
        parts = []
        for r, s in zip(here, scores):
            usable = position < len_ref[r]
            s = jnp.where(usable, s * SCALE2, FLOOR)
            high = jnp.max(s, axis=1, keepdims=True)
            p = jnp.where(usable, jnp.exp2(s - high), 0.0)
            parts.append((p, high, jnp.sum(p, axis=1, keepdims=True)))
        for r, (p, high, l) in zip(here, parts):
            o_ref[r] = _dot(p.astype(BF16), kv_ref[r, :, HEAD:]) / l
            lse_ref[r] = jnp.broadcast_to(high + jnp.log2(l), (GROUP, HEAD))


def _suffix(lengths, q, kv):
    rows, span = kv.shape[0], kv.shape[1]
    shape = jax.ShapeDtypeStruct((rows, GROUP, HEAD), F32)
    vmem = pl.BlockSpec(memory_space=pltpu.VMEM)
    return pl.pallas_call(
        _suffix_kernel,
        in_specs=[
            pl.BlockSpec(memory_space=pltpu.SMEM),
            vmem,
            pl.BlockSpec(memory_space=pltpu.HBM),
        ],
        out_specs=[vmem, vmem],
        out_shape=[shape, shape],
        scratch_shapes=[
            pltpu.VMEM(kv.shape, BF16),
            pltpu.SemaphoreType.DMA((8,)),
        ],
        compiler_params=_params(24, False),
        cost_estimate=pl.CostEstimate(
            flops=10**9, bytes_accessed=rows * span * 512, transcendentals=2**17
        ),
        name="suffix_attention",
    )(lengths, q.reshape(rows, GROUP, HEAD), _in_hbm(kv))


def _project_kernel(
    tenant_ref,
    recv_ref,
    o_ref,
    lse_ref,
    w_hbm,
    down_hbm,
    out_ref,
    att,
    low,
    w_ref,
    down_ref,
    sems,
):
    parts, rows = recv_ref.shape[0], recv_ref.shape[1]
    step = pl.program_id(0)
    width = w_ref.shape[2]

    def fetch_w(d):
        at = pl.multiple_of(d * width, HEAD)
        return pltpu.make_async_copy(
            w_hbm.at[:, pl.ds(at, width)], w_ref.at[d], sems.at[d]
        )

    fetch_down = pltpu.make_async_copy(down_hbm, down_ref, sems.at[w_ref.shape[0]])

    @pl.when(step == 0)
    def _():
        fetch_down.start()
        for d in range(w_ref.shape[0]):
            fetch_w(d).start()
        lane = _lane((rows, HEAD))
        own = jnp.zeros((rows, HEAD), F32)
        for g in range(GROUP):
            own = jnp.where(lane == g, lse_ref[:, g, :], own)
        lses = [own] + [
            _unpack3(recv_ref[w, :, GROUP * HEAD :].astype(F32)) for w in range(parts)
        ]
        top = functools.reduce(jnp.maximum, lses)
        weights = [jnp.exp2(x - top) for x in lses]
        z = functools.reduce(jnp.add, weights)
        weights = [x / z for x in weights]
        for g in range(GROUP):
            cols = slice(g * HEAD, (g + 1) * HEAD)
            acc = weights[0][:, g : g + 1] * o_ref[:, g, :]
            for w in range(parts):
                acc += weights[1 + w][:, g : g + 1] * recv_ref[w, :, cols].astype(F32)
            att[:, cols] = acc.astype(BF16)
        fetch_down.wait()
        reduced = _dot(att[...], down_ref[...])
        mine = _lane(reduced.shape) // RANK == tenant_ref[...]
        reduced = jnp.where(mine, reduced, 0.0)
        kept = reduced[:, :HEAD]
        for c in range(HEAD, reduced.shape[1], HEAD):
            kept = kept + reduced[:, c : c + HEAD]
        low[...] = kept.astype(BF16)

    fetch_w(step).wait()
    out_ref[0, :, :width] = _dot(att[...], w_ref[step]).astype(BF16)
    out_ref[0, :, width:] = low[...]


def _project(tenant, recv, o, lse, weight, down, parts):
    rows = recv.shape[1]
    depth, features = weight.shape
    width = features // parts

    def whole(shape):
        return pl.BlockSpec(shape, lambda d: (0,) * len(shape))

    return pl.pallas_call(
        _project_kernel,
        grid=(parts,),
        in_specs=[
            whole((rows, 1)),
            whole(recv.shape),
            whole(o.shape),
            whole(lse.shape),
            pl.BlockSpec(memory_space=pltpu.HBM),
            pl.BlockSpec(memory_space=pltpu.HBM),
        ],
        out_specs=pl.BlockSpec((1, rows, width + HEAD), lambda d: (d, 0, 0)),
        out_shape=jax.ShapeDtypeStruct((parts, rows, width + HEAD), BF16),
        scratch_shapes=[
            pltpu.VMEM((rows, GROUP * HEAD), BF16),
            pltpu.VMEM((rows, HEAD), BF16),
            pltpu.VMEM((parts, depth, width), BF16),
            pltpu.VMEM(down.shape, BF16),
            pltpu.SemaphoreType.DMA((parts + 1,)),
        ],
        compiler_params=_params(32),
        cost_estimate=pl.CostEstimate(
            flops=2 * rows * depth * features,
            bytes_accessed=2 * depth * features,
            transcendentals=0,
        ),
        name="project",
    )(tenant, recv, o, lse, _in_hbm(weight), _in_hbm(down))


def _finish_kernel(tenant_ref, recv_ref, up_ref, out_ref):
    parts, rows = recv_ref.shape[0], recv_ref.shape[1]
    width = out_ref.shape[1]
    total = recv_ref[0].astype(F32)
    for w in range(1, parts):
        total += recv_ref[w].astype(F32)
    depth = up_ref.shape[0]
    low = jnp.concatenate([total[:, width:]] * (depth // HEAD), axis=1)
    mine = _lane((rows, depth)) // RANK == tenant_ref[...]
    chosen = jnp.where(mine, low, 0.0).astype(BF16)
    out_ref[...] = (total[:, :width] + _dot(chosen, up_ref[...])).astype(BF16)


def _finish(tenant, recv, up):
    vmem = pl.BlockSpec(memory_space=pltpu.VMEM)
    return pl.pallas_call(
        _finish_kernel,
        in_specs=[vmem] * 3,
        out_specs=vmem,
        out_shape=jax.ShapeDtypeStruct((recv.shape[1], up.shape[1]), BF16),
        compiler_params=_params(16, False),
        name="finish",
    )(tenant, recv, up)


def per_device(
    queries,
    tenant,
    tenant_node_slot,
    suffix_length,
    system_prompt_cache,
    instruction_node_cache,
    suffix_cache,
    output_projection_weight,
    adapter_down_weight,
    adapter_up_weight,
):
    rows, width = queries.shape
    n_wide = lax.axis_size("wide")
    n_narrow = lax.axis_size("narrow")
    chips = n_wide // 2
    layers = chips // 2
    position = lax.axis_index("wide")
    layer, side, core = position // 4, position // 2 % 2, position % 2
    same_core = [[2 * j + c for j in range(chips)] for c in range(2)]
    sibling = [(i, i ^ 1) for i in range(n_wide)]
    n_slots = tenant_node_slot.shape[0]
    span = instruction_node_cache.shape[1]

    own = system_prompt_cache.reshape(-1, 2 * HEAD)
    sib = lax.ppermute(own, "wide", sibling)

    beside = lax.ppermute(queries, "wide", [(i, i ^ 2) for i in range(n_wide)])
    by_head = jnp.transpose(instruction_node_cache, (2, 0, 1, 3))
    beside, by_head = lax.optimization_barrier((beside, by_head))
    nodes = lax.all_to_all(by_head, "narrow", 0, 0, tiled=True)
    nodes = nodes.reshape(n_slots, span, 2 * HEAD)

    pair = jnp.where(
        side == 0,
        jnp.concatenate([queries, beside]),
        jnp.concatenate([beside, queries]),
    )
    pieces = [pair] + [
        lax.ppermute(pair, "wide", [((i + 4 * d) % n_wide, i) for i in range(n_wide)])
        for d in range(1, layers)
    ]
    order = (layer + jnp.arange(layers, dtype=jnp.int32)) % layers

    turned = lax.dynamic_slice_in_dim(
        jnp.concatenate([tenant, tenant]), layer * 4 * rows, n_wide * rows
    ).reshape(chips, 2, rows)
    mine = jnp.where(core == 0, turned[:, 0], turned[:, 1]).reshape(-1)

    kt, ve = _keys(own, sib)
    o_first, lse_first = _system(pieces[:1], kt, ve)
    *pieces[1:], lse_first[0] = lax.optimization_barrier((*pieces[1:], lse_first[0]))
    o_rest, lse_rest = _system(pieces[1:], kt, ve)
    o_sys, lse_sys = [*o_first, *o_rest], [*lse_first, *lse_rest]
    qs, back, table = _plan(tenant_node_slot, mine, pieces)

    o_suf, lse_suf = _suffix(
        suffix_length, queries, suffix_cache.reshape(rows, -1, 2 * HEAD)
    )
    nodes, lse_sys[-1] = lax.optimization_barrier((nodes, lse_sys[-1]))
    nodes_sib = lax.ppermute(nodes, "wide", sibling)
    sent = _node(table, order, qs, back, nodes, nodes_sib, o_sys, lse_sys)
    recv = lax.all_to_all(
        sent.reshape(chips, rows, -1),
        "wide",
        0,
        0,
        axis_index_groups=same_core,
        tiled=True,
    )
    my_tenant = lax.dynamic_slice_in_dim(tenant, position * rows, rows, 0)[:, None]
    parts = _project(
        my_tenant,
        recv,
        o_suf,
        lse_suf,
        output_projection_weight,
        adapter_down_weight,
        n_narrow,
    )
    parts = lax.all_to_all(parts, "narrow", 0, 0, tiled=True)
    return _finish(my_tenant, parts, adapter_up_weight)


def solution(mesh):
    return jax.shard_map(
        per_device,
        mesh=mesh,
        in_specs=(
            P("wide", "narrow"),
            P(),
            P(),
            P("wide"),
            P("wide", "narrow", None),
            P("narrow", "wide", None, None),
            P("wide", None, "narrow", None),
            P("narrow", None),
            P("narrow", None),
            P(None, "narrow"),
        ),
        out_specs=P("wide", "narrow"),
        check_vma=False,
    )
```

time: 163 us -> 120 us (0.74)
  waiting for transfers between devices: 47.3 us -> 17.4 us
  Pallas kernels: 63.6 us -> 51.2 us
    all_to_all x1, waiting for transfers between devices: 25.6 us -> 0.01 us  [per_device(): nodes = lax.all_to_all(by_head, 'narrow', 0, 0, tiled=True)]
    all_to_all x1 -> x0, waiting for transfers between devices: 13.9 us -> none  [per_device(): lax.all_to_all(jnp.broadcast_to(queries[None], (chips, rows, width)), 'wi...]
    ppermute x0 -> x4, starting transfers between devices: none -> 7.03 us  [the longest x3 5.37 us: per_device(): lax.ppermute(pair, 'wide', [((i + 4 * d) % n_wide, i) for i in range(n_wi...]
    all_to_all x1 -> x0, starting transfers between devices: 6.41 us -> none  [per_device(): lax.all_to_all(jnp.broadcast_to(queries[None], (chips, rows, width)), 'wi...]
    pallas_call x3 -> x6, Pallas kernels: 51.1 us -> 45.4 us  [the longest x2 24.6 us: _system(): pl.pallas_call(functools.partial(_system_kernel, count), grid=(GROUP // H...]
    pallas_call x1, Pallas kernels: 10.3 us -> 4.9 us  [_project(): pl.pallas_call(_project_kernel, grid=(parts,), in_specs=[whole((rows, 1))...]
    ppermute x0 -> x4, waiting for transfers between devices: none -> 5.04 us  [the longest x3 3.98 us: per_device(): lax.ppermute(pair, 'wide', [((i + 4 * d) % n_wide, i) for i in range(n_wi...]
    all_to_all x1, waiting for transfers between devices: 7.89 us -> 12.3 us  [per_device(): lax.all_to_all(sent.reshape(chips, rows, -1), 'wide', 0, 0, axis_index_gr...]
  transfers between devices with their start and end apart: 5 -> 8, of which waited for: 3 -> 4; matrix products, arithmetic and copies ran while one was open for 4% -> 5% of each run, Pallas kernels for 21% -> 28%
where the time goes in v1:
time: 120 us; the launch traced here: 119 us
  Pallas kernels  51.2 us (43%)
  blocking collectives  21 us (18%)
  starting transfers between devices  17.8 us (15%)
  waiting for transfers between devices  17.4 us (14%)
  local copies, waits for them, and re-layouts  10.2 us (8%)
  other arithmetic  1.71 us (1%)
    pallas_call x2, Pallas kernels, _system(): pl.pallas_call(functools.partial(_system_kernel, count), grid=(GROUP // H...  24.6 us
    all_to_all x1, blocking collectives, per_device(): parts = lax.all_to_all(parts, 'narrow', 0, 0, tiled=True)  21 us
    all_to_all x1, waiting for transfers between devices, per_device(): lax.all_to_all(sent.reshape(chips, rows, -1), 'wide', 0, 0, axis_index_gr...  12.3 us
    pallas_call x1, Pallas kernels, _node(): pl.pallas_call(functools.partial(_node_kernel, count), in_specs=[smem] *...  12 us
    unnamed x28, local copies, waits for them, and re-layouts  9.04 us
    all_to_all x1, starting transfers between devices, per_device(): nodes = lax.all_to_all(by_head, 'narrow', 0, 0, tiled=True)  7.15 us
    pallas_call x1, Pallas kernels, _suffix(): pl.pallas_call(_suffix_kernel, in_specs=[pl.BlockSpec(memory_space=pltpu....  5.47 us
    ppermute x3, starting transfers between devices, per_device(): lax.ppermute(pair, 'wide', [((i + 4 * d) % n_wide, i) for i in range(n_wi...  5.37 us
  transfers between devices with their start and end apart: 8, of which 4 were waited for; matrix products, arithmetic and copies ran while one was open for 5% of the time, Pallas kernels for 28%

profile of v1, /device:TPU:0, one launch (start us, length us, event | category | flops | bytes accessed | tf_op | source)
XLA Modules:
  0.0 119.4 jit_solution(1235278878504069140)
XLA Ops:
  0.0 1.7 %collective-permute-start = (bf16[64,1024]{1,0:T(8,128)(2,1)}, bf16[64,1024]{1,0:T(8,128)(2,1)S(1)}, u32[]{:S(2)}, u32[]{:S(2)}) collective-permute-start(bf16[64,1024]{1,0:T(8,128)(2,1)} %param.10), channel_id=1, source_target_pairs={{0,16},{8,24},{16,0},{24,8},{32,48},{40,56},{48,32},{56,40},{64,80... | collective-permute-start | bytes 393224 | tf_op jit(solution)/shard_map/ppermute | solution.py:564
  1.7 3.4 %copy.27 = bf16[4,128,8,256]{3,1,0,2:T(8,128)(2,1)} copy(bf16[4,128,8,256]{3,2,1,0:T(8,128)(2,1)} %param.15) | data formatting | bytes 4194304 | tf_op args[5]
  5.1 1.1 collective-permute-done
  6.8 7.1 %all-to-all-start = ((bf16[8,4,128,256]{3,2,1,0:T(8,128)(2,1)}), bf16[8,4,128,256]{3,2,1,0:T(8,128)(2,1)S(1)}, u32[]{:S(2)}, u32[]{:S(2)}) async-start(bf16[8,4,128,256]{3,2,1,0:T(8,128)(2,1)} %bitcast.19), calls=%async_computation | async-start | bytes 4194304 | tf_op jit(solution)/shard_map/all_to_all | solution.py:567
  13.9 1.0 maximum_select_fusion.refs_0_
  15.0 4.1 %collective-permute-start.1 = (bf16[128,1024]{1,0:T(8,128)(2,1)S(1)}, bf16[128,1024]{1,0:T(8,128)(2,1)S(1)}, u32[]{:S(2)}, u32[]{:S(2)}) collective-permute-start(bf16[128,1024]{1,0:T(8,128)(2,1)S(1)} %maximum_select_fusion.refs_0_), channel_id=1, source_target_pairs={{32,0},{40,8},{48,16},{56,24},{64,32},{72,40},{80,48},{88,56},{96,... | collective-permute-start | bytes 786440 | tf_op jit(solution)/shard_map/ppermute | solution.py:576
  19.1 1.3 %collective-permute-start.3 = (bf16[128,1024]{1,0:T(8,128)(2,1)S(1)}, bf16[128,1024]{1,0:T(8,128)(2,1)S(1)}, u32[]{:S(2)}, u32[]{:S(2)}) collective-permute-start(bf16[128,1024]{1,0:T(8,128)(2,1)S(1)} %maximum_select_fusion.refs_0_), channel_id=1, source_target_pairs={{96,0},{104,8},{112,16},{120,24},{0,32},{8,40},{16,48},{24,56},{32... | collective-permute-start | bytes 786440 | tf_op jit(solution)/shard_map/ppermute | solution.py:576
  20.4 1.8 %keys.1 = (bf16[128,4096]{1,0:T(8,128)(2,1)S(1)}, bf16[4096,256]{1,0:T(8,128)(2,1)S(1)}) custom-call(bf16[2048,256]{1,0:T(8,128)(2,1)S(1)} %bitcast.16, bf16[2048,256]{1,0:T(8,128)(2,1)} %collective-permute-done.4.sib_ref), custom_call_target="tpu_custom_call" | custom-call | bytes 5242880 | tf_op jit(solution)/shard_map/keys/pallas_call | solution.py:54
  22.2 7.1 %system_attention.2 = (f32[128,1024]{1,0:T(8,128)}, f32[128,128]{1,0:T(8,128)}) custom-call(bf16[128,1024]{1,0:T(8,128)(2,1)S(1)} %maximum_select_fusion.refs_0_, bf16[128,4096]{1,0:T(8,128)(2,1)S(1)} %get-tuple-element.29.refs_1_.refs_3_, bf16[4096,256]{1,0:T(8,128)(2,1)S(1)} %get-tuple-element.30.refs_2_.refs_4_), custom_call_target="tpu_custom_call" | custom-call | flops 3221225472 | bytes 3932160 | tf_op jit(solution)/shard_map/system_attention/pallas_call | solution.py:116
  29.9 3.4 %collective-permute-done.3.refs_3_.refs_2_ = bf16[128,1024]{1,0:T(8,128)(2,1)S(1)} collective-permute-done((bf16[128,1024]{1,0:T(8,128)(2,1)S(1)}, bf16[128,1024]{1,0:T(8,128)(2,1)S(1)}, u32[]{:S(2)}, u32[]{:S(2)}) %collective-permute-start.3) | collective-permute-done | bytes 262176 | tf_op jit(solution)/shard_map/ppermute | solution.py:576
  33.3 17.5 %system_attention.3 = (f32[128,1024]{1,0:T(8,128)}, f32[128,1024]{1,0:T(8,128)}, f32[128,1024]{1,0:T(8,128)}, f32[128,128]{1,0:T(8,128)}, f32[128,128]{1,0:T(8,128)}, /*index=5*/f32[128,128]{1,0:T(8,128)}) custom-call(bf16[128,1024]{1,0:T(8,128)(2,1)S(1)} %collective-permute-done.1.refs_1_.refs_0_, ...), custom_call_target="tpu_custom_call" | custom-call | flops 9663676416 | bytes 5505024 | tf_op jit(solution)/shard_map/system_attention/pallas_call | solution.py:116
  50.8 0.7 copy-done.3
  52.2 0.7 copy-done.7
  54.5 0.9 copy-done.4
  55.5 0.9 copy-done.6
  56.4 0.9 copy-done.8
  57.4 1.5 %plan.1 = (bf16[512,1024]{1,0:T(8,128)(2,1)S(1)}, bf16[512,512]{1,0:T(8,128)(2,1)S(1)}, s32[8,128]{1,0:T(8,128)S(1)}) custom-call(s32[32,1]{1,0:T(8,128)S(1)} %copy.21.slot_ref, s32[1,512]{1,0:T(1,128)S(1)} %select_n.72.row_ref, s32[512,1]{1,0:T(8,128)S(1)} %select_n.79.col_ref, bf16[128,1024]{1,0:T(8,128)(2,1)S(1)} %maximum_select_fusion.refs_0_, ...), custom_call_target="tpu_custom_call" | custom-call | flops 536870912 | bytes 3145728 | tf_op jit(solution)/shard_map/plan/pallas_call | solution.py:215
  58.9 12.0 %node_attention.1 = bf16[512,1152]{1,0:T(8,128)(2,1)} custom-call(s32[8,128]{1,0:T(8,128)S(1)} %get-tuple-element.35.table, s32[4]{0:T(128)S(1)} %and_select_fusion.order, bf16[512,1024]{1,0:T(8,128)(2,1)S(1)} %get-tuple-element.36.qs, bf16[512,512]{1,0:T(8,128)(2,1)S(1)} %get-tuple-element.37.back_ref, bf16[32,128,256]{2,1,0:T(8,128)(2,1)S(1)} %bitcast.14, ...), custom_call_target="tpu_custom_call" | custom-call | flops 2000000000 | bytes 8388608 | tf_op jit(solution)/shard_map/node_attention/pallas_call | solution.py:331
  70.9 3.6 %all-to-all-start.1 = ((bf16[8,64,1152]{2,1,0:T(8,128)(2,1)}), bf16[8,64,1152]{2,1,0:T(8,128)(2,1)S(1)}, u32[]{:S(2)}, u32[]{:S(2)}) async-start(bf16[8,64,1152]{2,1,0:T(8,128)(2,1)} %bitcast.5), calls=%async_computation.1 | async-start | bytes 2359296 | tf_op jit(solution)/shard_map/all_to_all | solution.py:599
  74.7 5.5 %suffix_attention.1 = (f32[64,8,128]{2,1,0:T(8,128)S(1)}, f32[64,8,128]{2,1,0:T(8,128)S(1)}) custom-call(s32[64]{0:T(128)S(1)} %copy-done.2, bf16[64,8,128]{2,1,0:T(8,128)(2,1)S(1)} %bitcast.17, bf16[64,256,256]{2,1,0:T(8,128)(2,1)} %bitcast.18), custom_call_target="tpu_custom_call" | custom-call | flops 1000000000 | bytes 8388608 | tf_op jit(solution)/shard_map/suffix_attention/pallas_call | solution.py:391
  80.2 12.3 %all-to-all-done.1.recv_ref = bf16[8,64,1152]{2,1,0:T(8,128)(2,1)S(1)} async-done(((bf16[8,64,1152]{2,1,0:T(8,128)(2,1)}), bf16[8,64,1152]{2,1,0:T(8,128)(2,1)S(1)}, u32[]{:S(2)}, u32[]{:S(2)}) %all-to-all-start.1) | async-done | bytes 1179680 | tf_op jit(solution)/shard_map/all_to_all | solution.py:599
  92.5 4.9 %project.1 = bf16[8,64,768]{2,1,0:T(8,128)(2,1)S(1)} custom-call(s32[64,1]{1,0:T(8,128)S(1)} %copy.24.tenant_ref, bf16[8,64,1152]{2,1,0:T(8,128)(2,1)S(1)} %all-to-all-done.1.recv_ref, f32[64,8,128]{2,1,0:T(8,128)S(1)} %get-tuple-element.49.o_ref, f32[64,8,128]{2,1,0:T(8,128)S(1)} %get-tuple-element.50.lse_ref, bf16[1024,5120]{1,0:T(8,128)(2,1)} %w_hbm.1, ...), custom_call_target="tpu_custom_call" | custom-call | flops 671088640 | bytes 10485760 | tf_op jit(solution)/shard_map/project/pallas_call | solution.py:482
  97.4 21.0 %all_to_all.15.recv_ref = bf16[8,64,768]{2,1,0:T(8,128)(2,1)S(1)} all-to-all(bf16[8,64,768]{2,1,0:T(8,128)(2,1)S(1)} %project.1), channel_id=1, replica_groups=mesh['wide'=16,'narrow'=8] {'narrow'}, dimensions={0} | all-to-all | bytes 1572864 | tf_op jit(solution)/shard_map/all_to_all | solution.py:617
  118.4 0.9 finish.1
  (40 shorter events, 3.8 us)
Async XLA Ops:
  0.0 20.3 %collective-permute-start.4 = (bf16[2048,256]{1,0:T(8,128)(2,1)}, bf16[2048,256]{1,0:T(8,128)(2,1)}, u32[]{:S(2)}, u32[]{:S(2)}) collective-permute-start(bf16[2048,256]{1,0:T(8,128)(2,1)} %bitcast.15), channel_id=1, source_target_pairs={{0,8},{8,0},{16,24},{24,16},{32,40},{40,32},{48,56},{56,48},{64,72... | collective-permute-start | bytes 3145736 | tf_op jit(solution)/shard_map/ppermute | solution.py:562
  0.0 6.1 %collective-permute-start = (bf16[64,1024]{1,0:T(8,128)(2,1)}, bf16[64,1024]{1,0:T(8,128)(2,1)S(1)}, u32[]{:S(2)}, u32[]{:S(2)}) collective-permute-start(bf16[64,1024]{1,0:T(8,128)(2,1)} %param.10), channel_id=1, source_target_pairs={{0,16},{8,24},{16,0},{24,8},{32,48},{40,56},{48,32},{56,40},{64,80... | collective-permute-start | bytes 393224 | tf_op jit(solution)/shard_map/ppermute | solution.py:564
  6.1 0.7 copy-start.10
  6.8 7.2 %copy-start.9 = (bf16[64,1024]{1,0:T(8,128)(2,1)S(1)}, bf16[64,1024]{1,0:T(8,128)(2,1)}, u32[]{:S(2)}) copy-start(bf16[64,1024]{1,0:T(8,128)(2,1)} %param.10) | copy-start | bytes 393220
  6.8 13.6 %copy-start = (bf16[2048,1,256]{2,0,1:T(8,128)(2,1)S(1)}, bf16[2048,1,256]{2,0,1:T(8,128)(2,1)}, u32[]{:S(2)}) copy-start(bf16[2048,1,256]{2,0,1:T(8,128)(2,1)} %param.14) | copy-start | bytes 3145732
  6.8 46.1 %all-to-all-start = ((bf16[8,4,128,256]{3,2,1,0:T(8,128)(2,1)}), bf16[8,4,128,256]{3,2,1,0:T(8,128)(2,1)S(1)}, u32[]{:S(2)}, u32[]{:S(2)}) async-start(bf16[8,4,128,256]{3,2,1,0:T(8,128)(2,1)} %bitcast.19), calls=%async_computation | async-start | bytes 4194304 | tf_op jit(solution)/shard_map/all_to_all | solution.py:567
  15.0 14.9 %collective-permute-start.1 = (bf16[128,1024]{1,0:T(8,128)(2,1)S(1)}, bf16[128,1024]{1,0:T(8,128)(2,1)S(1)}, u32[]{:S(2)}, u32[]{:S(2)}) collective-permute-start(bf16[128,1024]{1,0:T(8,128)(2,1)S(1)} %maximum_select_fusion.refs_0_), channel_id=1, source_target_pairs={{32,0},{40,8},{48,16},{56,24},{64,32},{72,40},{80,48},{88,56},{96,... | collective-permute-start | bytes 786440 | tf_op jit(solution)/shard_map/ppermute | solution.py:576
  19.1 10.8 %collective-permute-start.2 = (bf16[128,1024]{1,0:T(8,128)(2,1)S(1)}, bf16[128,1024]{1,0:T(8,128)(2,1)S(1)}, u32[]{:S(2)}, u32[]{:S(2)}) collective-permute-start(bf16[128,1024]{1,0:T(8,128)(2,1)S(1)} %maximum_select_fusion.refs_0_), channel_id=1, source_target_pairs={{64,0},{72,8},{80,16},{88,24},{96,32},{104,40},{112,48},{120,56},{... | collective-permute-start | bytes 786440 | tf_op jit(solution)/shard_map/ppermute | solution.py:576
  19.1 14.2 %collective-permute-start.3 = (bf16[128,1024]{1,0:T(8,128)(2,1)S(1)}, bf16[128,1024]{1,0:T(8,128)(2,1)S(1)}, u32[]{:S(2)}, u32[]{:S(2)}) collective-permute-start(bf16[128,1024]{1,0:T(8,128)(2,1)S(1)} %maximum_select_fusion.refs_0_), channel_id=1, source_target_pairs={{96,0},{104,8},{112,16},{120,24},{0,32},{8,40},{16,48},{24,56},{32... | collective-permute-start | bytes 786440 | tf_op jit(solution)/shard_map/ppermute | solution.py:576
  33.3 19.6 %copy-start.11 = (s32[1024]{0:T(1024)S(1)}, s32[1024]{0:T(1024)}, u32[]{:S(2)}) copy-start(s32[1024]{0:T(1024)} %param.11) | copy-start | bytes 12292
  33.3 21.1 %copy-start.12 = (s32[32]{0:T(128)S(1)}, s32[32]{0:T(128)}, u32[]{:S(2)}) copy-start(s32[32]{0:T(128)} %param.12) | copy-start | bytes 388
  50.8 0.7 copy-start.3
  51.5 0.7 copy-start.5
  52.2 0.7 copy-start.7
  52.9 6.0 %collective-permute-start.5 = (bf16[32,128,256]{2,1,0:T(8,128)(2,1)S(1)}, bf16[32,128,256]{2,1,0:T(8,128)(2,1)}, u32[]{:S(2)}, u32[]{:S(2)}) collective-permute-start(bf16[32,128,256]{2,1,0:T(8,128)(2,1)S(1)} %bitcast.13), channel_id=1, source_target_pairs={{0,8},{8,0},{16,24},{24,16},{32,40},{40,32},{48,56},{56,48},{64,72... | collective-permute-start | bytes 6291464 | tf_op jit(solution)/shard_map/ppermute | solution.py:597
  54.5 1.0 copy-start.4
  55.5 0.9 copy-start.6
  56.4 0.9 copy-start.8
  70.9 3.8 %copy-start.2 = (s32[64]{0:T(128)S(1)}, s32[64]{0:T(128)}, u32[]{:S(2)}) copy-start(s32[64]{0:T(128)} %len_ref.1) | copy-start | bytes 772
  70.9 21.6 %all-to-all-start.1 = ((bf16[8,64,1152]{2,1,0:T(8,128)(2,1)}), bf16[8,64,1152]{2,1,0:T(8,128)(2,1)S(1)}, u32[]{:S(2)}, u32[]{:S(2)}) async-start(bf16[8,64,1152]{2,1,0:T(8,128)(2,1)} %bitcast.5), calls=%async_computation.1 | async-start | bytes 2359296 | tf_op jit(solution)/shard_map/all_to_all | solution.py:599
  92.5 25.9 %copy-start.1 = (bf16[512,640]{1,0:T(8,128)(2,1)S(1)}, bf16[512,640]{1,0:T(8,128)(2,1)}, u32[]{:S(2)}) copy-start(bf16[512,640]{1,0:T(8,128)(2,1)} %up_ref.1) | copy-start | bytes 1966084

commit v2 on v1

--- a/solution.py
+++ b/solution.py
@@ -17,7 +17,7 @@
 KEY_BLOCK = 2048
 HEADS_AT_ONCE = 2
 VISIT_ROWS = 16
-VISIT_UNROLL = 8
+VISIT_UNROLL = 16
 
 
 def _params(mib, grid=True):
@@ -29,6 +29,10 @@
 
 def _in_hbm(x):
     return pltpu.with_memory_space_constraint(x, pltpu.HBM)
+
+
+def _in_vmem(x):
+    return pltpu.with_memory_space_constraint(x, pltpu.VMEM)
 
 
 def _lane(shape):
@@ -56,8 +60,8 @@
         in_specs=[vmem] * 2,
         out_specs=[vmem] * 2,
         out_shape=[
-            jax.ShapeDtypeStruct((HEAD, n), BF16),
-            jax.ShapeDtypeStruct((n, 2 * HEAD), BF16),
+            pltpu.VMEM((HEAD, n), BF16),
+            pltpu.VMEM((n, 2 * HEAD), BF16),
         ],
         compiler_params=_params(16, False),
         cost_estimate=pl.CostEstimate(
@@ -68,10 +72,17 @@
 
 
 def _system_kernel(count, *refs):
-    q_refs, (kt, ve) = refs[:count], refs[count : count + 2]
-    o_refs, lse_refs = refs[count + 2 : 2 * count + 2], refs[2 * count + 2 :]
-    step = pl.program_id(0)
-    rows, keys = q_refs[0].shape[0], kt.shape[1]
+    q_hbm, (kt, ve) = refs[:count], refs[count : count + 2]
+    o_hbm, lse_hbm = refs[count + 2 : 2 * count + 2], refs[2 * count + 2 : 3 * count + 2]
+    q_buf, o_buf, lse_buf, sems = refs[3 * count + 2 :]
+    steps = GROUP // HEADS_AT_ONCE
+    rows, keys = q_buf.shape[1], kt.shape[1]
+    first = [
+        pltpu.make_async_copy(q_hbm[b], q_buf.at[b], sems.at[b, steps])
+        for b in range(count)
+    ]
+    for copy in first:
+        copy.start()
     lane = _lane((rows, HEAD))
     items = [
         (h, b, k)
@@ -79,59 +90,89 @@
         for b in range(count)
         for k in range(0, keys, KEY_BLOCK)
     ]
-
-    def score(item):
-        h, b, k = item
-        q = q_refs[b][:, h * HEAD : (h + 1) * HEAD]
-        return _dot(q, kt[:, k : k + KEY_BLOCK])
-
-    top, total = {}, {}
-    ahead = score(items[0])
-    for i, (h, b, k) in enumerate(items):
-        s = ahead
-        if i + 1 < len(items):
-            ahead = score(items[i + 1])
-        high = jnp.max(s, axis=1, keepdims=True) * SCALE2
-        if (h, b) in top:
-            high = jnp.maximum(high, top[h, b])
-        p = jnp.exp2(s * SCALE2 - high).astype(BF16)
-        r = _dot(p, ve[k : k + KEY_BLOCK, :])
-        if (h, b) in top:
-            r = total[h, b] * jnp.exp2(top[h, b] - high) + r
-        top[h, b], total[h, b] = high, r
     for b in range(count):
-        packed = jnp.where(step == 0, 0.0, lse_refs[b][...])
-        for h in range(HEADS_AT_ONCE):
-            l = total[h, b][:, HEAD:]
-            o_refs[b][:, h * HEAD : (h + 1) * HEAD] = total[h, b][:, :HEAD] / l
-            lse = top[h, b] + jnp.log2(l)
-            packed = jnp.where(lane == step * HEADS_AT_ONCE + h, lse, packed)
-        lse_refs[b][...] = packed
+        lse_buf[b] = jnp.zeros((rows, HEAD), F32)
+    for copy in first:
+        copy.wait()
+
+    def send(b, step):
+        width = HEADS_AT_ONCE * HEAD
+        at = pl.ds(pl.multiple_of(step * width, width), width)
+        return pltpu.make_async_copy(
+            o_buf.at[b, :, at], o_hbm[b].at[:, at], sems.at[b, step]
+        )
+
+    def some_heads(step, carry):
+        def columns(h):
+            at = pl.multiple_of((step * HEADS_AT_ONCE + h) * HEAD, HEAD)
+            return pl.ds(at, HEAD)
+
+        def score(item):
+            h, b, k = item
+            return _dot(q_buf[b, :, columns(h)], kt[:, k : k + KEY_BLOCK])
+
+        top, total = {}, {}
+        ahead = score(items[0])
+        for i, (h, b, k) in enumerate(items):
+            s = ahead
+            if i + 1 < len(items):
+                ahead = score(items[i + 1])
+            high = jnp.max(s, axis=1, keepdims=True) * SCALE2
+            if (h, b) in top:
+                high = jnp.maximum(high, top[h, b])
+            p = jnp.exp2(s * SCALE2 - high).astype(BF16)
+            r = _dot(p, ve[k : k + KEY_BLOCK, :])
+            if (h, b) in top:
+                r = total[h, b] * jnp.exp2(top[h, b] - high) + r
+            top[h, b], total[h, b] = high, r
+        for b in range(count):
+            packed = lse_buf[b]
+            for h in range(HEADS_AT_ONCE):
+                l = total[h, b][:, HEAD:]
+                o_buf[b, :, columns(h)] = total[h, b][:, :HEAD] / l
+                lse = top[h, b] + jnp.log2(l)
+                packed = jnp.where(lane == step * HEADS_AT_ONCE + h, lse, packed)
+            lse_buf[b] = packed
+            send(b, step).start()
+        return carry
+
+    lax.fori_loop(0, steps, some_heads, 0)
+    last = [
+        pltpu.make_async_copy(lse_buf.at[b], lse_hbm[b], sems.at[b, steps])
+        for b in range(count)
+    ]
+    for copy in last:
+        copy.start()
+    for b in range(count):
+        for step in range(steps):
+            send(b, step).wait()
+        last[b].wait()
 
 
 def _system(qs, kt, ve):
     count, rows, keys = len(qs), qs[0].shape[0], ve.shape[0]
-    heads = pl.BlockSpec((rows, HEADS_AT_ONCE * HEAD), lambda g: (0, g))
-    fixed = pl.BlockSpec((rows, HEAD), lambda g: (0, 0))
+    vmem = pl.BlockSpec(memory_space=pltpu.VMEM)
+    hbm = pl.BlockSpec(memory_space=pltpu.HBM)
     outs = pl.pallas_call(
         functools.partial(_system_kernel, count),
-        grid=(GROUP // HEADS_AT_ONCE,),
-        in_specs=[heads] * count
-        + [
-            pl.BlockSpec(kt.shape, lambda g: (0, 0)),
-            pl.BlockSpec(ve.shape, lambda g: (0, 0)),
-        ],
-        out_specs=[heads] * count + [fixed] * count,
+        in_specs=[hbm] * count + [vmem] * 2,
+        out_specs=[hbm] * (2 * count),
         out_shape=[pltpu.HBM((rows, GROUP * HEAD), F32)] * count
         + [pltpu.HBM((rows, HEAD), F32)] * count,
-        compiler_params=_params(32),
+        scratch_shapes=[
+            pltpu.VMEM((count, rows, GROUP * HEAD), BF16),
+            pltpu.VMEM((count, rows, GROUP * HEAD), F32),
+            pltpu.VMEM((count, rows, HEAD), F32),
+            pltpu.SemaphoreType.DMA((count, GROUP // HEADS_AT_ONCE + 1)),
+        ],
+        compiler_params=_params(24, False),
         cost_estimate=pl.CostEstimate(
             flops=6 * count * rows * GROUP * keys * HEAD,
             bytes_accessed=count * rows * 6 * GROUP * HEAD + 6 * keys * HEAD,
             transcendentals=count * rows * GROUP * keys,
         ),
         name="system_attention",
-    )(*qs, kt, ve)
+    )(*map(_in_hbm, qs), *map(_in_vmem, [kt, ve]))
     return list(outs[:count]), list(outs[count:])
 
 
@@ -155,19 +196,42 @@
     return x + (pltpu.roll(x, HEAD - GROUP, 1) + pltpu.roll(x, HEAD - 2 * GROUP, 1))
 
 
-def _plan_kernel(slot_ref, row_ref, col_ref, *refs):
-    q_refs, (qs_ref, back_ref, table_ref) = refs[:-3], refs[-3:]
+def _plan_kernel(place, slot_ref, tenant_ref, *refs):
+    q_hbm, (qs_ref, back_ref, table_ref, q_buf, sems) = refs[:-5], refs[-5:]
+    fetches = [
+        pltpu.make_async_copy(ref, q_buf.at[i], sems.at[i])
+        for i, ref in enumerate(q_hbm)
+    ]
+    for fetch in fetches:
+        fetch.start()
     rows = qs_ref.shape[0]
-    piece = q_refs[0].shape[0]
-    tenants = slot_ref.shape[0]
+    piece = q_buf.shape[1]
+    tenants = slot_ref.shape[1]
     width = table_ref.shape[1]
-    t_row, t_col = row_ref[...], col_ref[...]
 
     def iota(shape, dim):
         return lax.broadcasted_iota(jnp.int32, shape, dim)
 
     def count(where, axis):
         return jnp.sum(where.astype(jnp.int32), axis=axis, keepdims=True)
+
+    chips, both = tenant_ref.shape
+    layer, core = place[0], place[1]
+    turned = pltpu.roll(tenant_ref[...], (chips - 2 * layer) % chips, 0)
+    turned = pltpu.roll(turned, core * (both // 2), 1)
+    spread = jnp.concatenate(
+        [
+            jnp.broadcast_to(turned[j : j + 1, :], (both // 2, both))
+            for j in range(chips)
+        ],
+        axis=0,
+    )
+    own_lane = iota(spread.shape, 1) == iota(spread.shape, 0) % (both // 2)
+    t_col = jnp.sum(jnp.where(own_lane, spread, 0), axis=1, keepdims=True)
+    square = iota((rows, rows), 0) == iota((rows, rows), 1)
+    t_row = jnp.sum(jnp.where(square, t_col, 0), axis=0, keepdims=True)
+    square = iota((tenants, tenants), 0) == iota((tenants, tenants), 1)
+    slot_col = jnp.sum(jnp.where(square, slot_ref[...], 0), axis=1, keepdims=True)
 
     key_row = t_row * rows + iota((1, rows), 1)
     key_col = t_col * rows + iota((rows, 1), 0)
@@ -175,9 +239,11 @@
     rank_col = count(key_row < key_col, 1)
     to_sorted = (iota((rows, rows), 0) == rank_row).astype(F32).astype(BF16)
     back_ref[...] = (iota((rows, rows), 1) == rank_col).astype(F32).astype(BF16)
+    for fetch in fetches:
+        fetch.wait()
     qs_ref[...] = sum(
-        _dot(to_sorted[:, i * piece : (i + 1) * piece], ref[...])
-        for i, ref in enumerate(q_refs)
+        _dot(to_sorted[:, i * piece : (i + 1) * piece], q_buf[i])
+        for i in range(len(fetches))
     ).astype(BF16)
 
     def visits_of(low, high):
@@ -199,7 +265,7 @@
     table_ref[...] = jnp.concatenate(
         [
             pick(first - start + lane),
-            pick(slot_ref[...]),
+            pick(slot_col),
             pick(low),
             pick(high),
             jnp.broadcast_to(jnp.sum(n, axis=0, keepdims=True), (1, width)),
@@ -209,17 +275,24 @@
     )
 
 
-def _plan(slots, mine, qs):
-    rows, width = mine.shape[0], qs[0].shape[1]
+def _plan(place, slots, tenant, qs):
+    rows, width = sum(q.shape[0] for q in qs), qs[0].shape[1]
+    chips = 2 * len(qs)
     vmem = pl.BlockSpec(memory_space=pltpu.VMEM)
     return pl.pallas_call(
         _plan_kernel,
-        in_specs=[vmem] * (3 + len(qs)),
+        in_specs=[pl.BlockSpec(memory_space=pltpu.SMEM)]
+        + [vmem] * 2
+        + [pl.BlockSpec(memory_space=pltpu.HBM)] * len(qs),
         out_specs=[vmem] * 3,
         out_shape=[
-            jax.ShapeDtypeStruct((rows, width), BF16),
-            jax.ShapeDtypeStruct((rows, rows), BF16),
+            pltpu.VMEM((rows, width), BF16),
+            pltpu.VMEM((rows, rows), BF16),
             jax.ShapeDtypeStruct((8, HEAD), jnp.int32),
+        ],
+        scratch_shapes=[
+            pltpu.VMEM((len(qs), *qs[0].shape), BF16),
+            pltpu.SemaphoreType.DMA((len(qs),)),
         ],
         compiler_params=_params(16, False),
         cost_estimate=pl.CostEstimate(
@@ -228,19 +301,18 @@
             transcendentals=0,
         ),
         name="plan",
-    )(slots[:, None], mine[None, :], mine[:, None], *qs)
-
-
-def _node_kernel(count, table, order, qs, back_ref, own_ref, sib_ref, *refs):
+    )(place, slots[None, :], tenant.reshape(chips, -1), *map(_in_hbm, qs))
+
+
+def _node_kernel(count, table, place, qs, back_ref, own_ref, sib_ref, *refs):
     o_hbm, lse_hbm = refs[:count], refs[count : 2 * count]
-    out_ref, on, lse_n, o_buf, lse_buf, sems = refs[2 * count :]
-    fetches = [
-        pltpu.make_async_copy(src, dst, sems.at[i])
-        for i, (src, dst) in enumerate(
-            [(o_hbm[i], o_buf.at[i]) for i in range(count)]
-            + [(lse_hbm[i], lse_buf.at[i]) for i in range(count)]
-        )
-    ]
+    out_ref, on, lse_n, o_buf, lse_buf, done, sems = refs[2 * count :]
+    fetches = []
+    for i in range(count):
+        fetches += [
+            pltpu.make_async_copy(o_hbm[i], o_buf.at[i], sems.at[i]),
+            pltpu.make_async_copy(lse_hbm[i], lse_buf.at[i], sems.at[count + i]),
+        ]
     for fetch in fetches:
         fetch.start()
     vr = VISIT_ROWS
@@ -299,30 +371,36 @@
 
     lax.fori_loop(0, (table[4, 0] + VISIT_UNROLL - 1) // VISIT_UNROLL, step, 0)
 
-    for fetch in fetches:
-        fetch.wait()
     packed_lse = _pack3(lse_n[...])
-    piece = o_buf.shape[1]
+    piece = done.shape[1]
+    sends = []
     for i in range(count):
         back = back_ref[i * piece : (i + 1) * piece, :]
-        to = pl.ds(pl.multiple_of(order[i] * piece, piece), piece)
         lse_node = _unpack3(_dot(back, packed_lse))
+        o_node = _dot(back, on[...])
+        fetches[2 * i].wait()
+        fetches[2 * i + 1].wait()
         lse_sys = lse_buf[i]
         top = jnp.maximum(lse_sys, lse_node)
         w_sys, w_node = jnp.exp2(lse_sys - top), jnp.exp2(lse_node - top)
         z = w_sys + w_node
-        out_ref[to, GROUP * HEAD :] = _pack3(top + jnp.log2(z))
-        w_sys, w_node = w_sys / z, w_node / z
+        done[i, :, GROUP * HEAD :] = _pack3(top + jnp.log2(z))
+        w_node = w_node / z
         for g in range(GROUP):
             cols = slice(g * HEAD, (g + 1) * HEAD)
-            o_node = _dot(back, on[:, cols])
-            out_ref[to, cols] = (
-                w_sys[:, g : g + 1] * o_buf[i, :, cols]
-                + w_node[:, g : g + 1] * o_node
-            ).astype(BF16)
-
-
-def _node(table, order, qs, back, own, sib, o_sys, lse_sys):
+            o_sys = o_buf[i, :, cols]
+            o = o_sys + w_node[:, g : g + 1] * (o_node[:, cols] - o_sys)
+            done[i, :, cols] = o.astype(BF16)
+        layer = lax.rem(place[0] + i, count)
+        to = pl.ds(pl.multiple_of(layer * piece, piece), piece)
+        send = pltpu.make_async_copy(done.at[i], out_ref.at[to], sems.at[2 * count + i])
+        send.start()
+        sends.append(send)
+    for send in sends:
+        send.wait()
+
+
+def _node(table, place, qs, back, own, sib, o_sys, lse_sys):
     rows, count = qs.shape[0], len(o_sys)
     smem = pl.BlockSpec(memory_space=pltpu.SMEM)
     hbm = pl.BlockSpec(memory_space=pltpu.HBM)
@@ -331,21 +409,27 @@
     return pl.pallas_call(
         functools.partial(_node_kernel, count),
         in_specs=[smem] * 2 + [vmem] * 4 + [hbm] * (2 * count),
-        out_specs=vmem,
-        out_shape=jax.ShapeDtypeStruct((rows, (GROUP + 1) * HEAD), BF16),
+        out_specs=hbm,
+        out_shape=pltpu.HBM((rows, (GROUP + 1) * HEAD), BF16),
         scratch_shapes=[
             pltpu.VMEM((rows, GROUP * HEAD), BF16),
             pltpu.VMEM((rows, HEAD), F32),
             pltpu.VMEM((count, piece, GROUP * HEAD), F32),
             pltpu.VMEM((count, piece, HEAD), F32),
-            pltpu.SemaphoreType.DMA((2 * count,)),
+            pltpu.VMEM((count, piece, (GROUP + 1) * HEAD), BF16),
+            pltpu.SemaphoreType.DMA((3 * count,)),
         ],
         compiler_params=_params(24, False),
         cost_estimate=pl.CostEstimate(
             flops=2 * 10**9, bytes_accessed=8 * 2**20, transcendentals=2**20
         ),
         name="node_attention",
-    )(table, order, qs, back, own, sib, *map(_in_hbm, [*o_sys, *lse_sys]))
+    )(
+        table,
+        place,
+        *map(_in_vmem, [qs, back, own, sib]),
+        *map(_in_hbm, [*o_sys, *lse_sys]),
+    )
 
 
 def _suffix_kernel(len_ref, q_ref, kv_hbm, o_ref, lse_ref, kv_ref, sems):
@@ -563,7 +647,8 @@
 
     beside = lax.ppermute(queries, "wide", [(i, i ^ 2) for i in range(n_wide)])
     by_head = jnp.transpose(instruction_node_cache, (2, 0, 1, 3))
-    beside, by_head = lax.optimization_barrier((beside, by_head))
+    place = jnp.stack([layer, core])
+    beside, by_head, place = lax.optimization_barrier((beside, by_head, place))
     nodes = lax.all_to_all(by_head, "narrow", 0, 0, tiled=True)
     nodes = nodes.reshape(n_slots, span, 2 * HEAD)
 
@@ -576,26 +661,21 @@
         lax.ppermute(pair, "wide", [((i + 4 * d) % n_wide, i) for i in range(n_wide)])
         for d in range(1, layers)
     ]
-    order = (layer + jnp.arange(layers, dtype=jnp.int32)) % layers
-
-    turned = lax.dynamic_slice_in_dim(
-        jnp.concatenate([tenant, tenant]), layer * 4 * rows, n_wide * rows
-    ).reshape(chips, 2, rows)
-    mine = jnp.where(core == 0, turned[:, 0], turned[:, 1]).reshape(-1)
-
     kt, ve = _keys(own, sib)
-    o_first, lse_first = _system(pieces[:1], kt, ve)
-    *pieces[1:], lse_first[0] = lax.optimization_barrier((*pieces[1:], lse_first[0]))
-    o_rest, lse_rest = _system(pieces[1:], kt, ve)
-    o_sys, lse_sys = [*o_first, *o_rest], [*lse_first, *lse_rest]
-    qs, back, table = _plan(tenant_node_slot, mine, pieces)
+    o_a, lse_a = _system(pieces[:1], kt, ve)
+    *pieces[1:], lse_a[0] = lax.optimization_barrier((*pieces[1:], lse_a[0]))
+    o_b, lse_b = _system(pieces[1:], kt, ve)
+    o_sys, lse_sys = [*o_a, *o_b], [*lse_a, *lse_b]
+    nodes, lse_sys[-1], *pieces = lax.optimization_barrier(
+        (nodes, lse_sys[-1], *pieces)
+    )
+    nodes_sib = lax.ppermute(nodes, "wide", sibling)
+    qs, back, table = _plan(place, tenant_node_slot, tenant, pieces)
 
     o_suf, lse_suf = _suffix(
         suffix_length, queries, suffix_cache.reshape(rows, -1, 2 * HEAD)
     )
-    nodes, lse_sys[-1] = lax.optimization_barrier((nodes, lse_sys[-1]))
-    nodes_sib = lax.ppermute(nodes, "wide", sibling)
-    sent = _node(table, order, qs, back, nodes, nodes_sib, o_sys, lse_sys)
+    sent = _node(table, place, qs, back, nodes, nodes_sib, o_sys, lse_sys)
     recv = lax.all_to_all(
         sent.reshape(chips, rows, -1),
         "wide",

time: 120 us -> 112 us (0.933)
  local copies, waits for them, and re-layouts: 10.2 us -> 4.37 us
  other arithmetic: 1.71 us -> 0.13 us
    unnamed x28 -> x22, local copies, waits for them, and re-layouts: 9.04 us -> 4.19 us
    pallas_call x3, Pallas kernels: 26.1 us -> 29.7 us  [the longest x2 26.5 us: _system(): pl.pallas_call(functools.partial(_system_kernel, count), in_specs=[hbm] *...]
    pallas_call x1, Pallas kernels: 12 us -> 8.78 us  [_node(): pl.pallas_call(functools.partial(_node_kernel, count), in_specs=[smem] *...]
  transfers between devices with their start and end apart: 8 -> 8, of which waited for: 4 -> 4; matrix products, arithmetic and copies ran while one was open for 5% -> 3% of each run, Pallas kernels for 28% -> 33%
where the time goes in v2:
time: 112 us
  Pallas kernels  51.6 us (46%)
  blocking collectives  20.6 us (18%)
  starting transfers between devices  17.8 us (16%)
  waiting for transfers between devices  16.9 us (15%)
  local copies, waits for them, and re-layouts  4.37 us (4%)
    pallas_call x2, Pallas kernels, _system(): pl.pallas_call(functools.partial(_system_kernel, count), in_specs=[hbm] *...  26.5 us
    all_to_all x1, blocking collectives, per_device(): parts = lax.all_to_all(parts, 'narrow', 0, 0, tiled=True)  20.6 us
    all_to_all x1, waiting for transfers between devices, per_device(): lax.all_to_all(sent.reshape(chips, rows, -1), 'wide', 0, 0, axis_index_gr...  12 us
    pallas_call x1, Pallas kernels, _node(): pl.pallas_call(functools.partial(_node_kernel, count), in_specs=[smem] *...  8.78 us
    all_to_all x1, starting transfers between devices, per_device(): nodes = lax.all_to_all(by_head, 'narrow', 0, 0, tiled=True)  7.15 us
    pallas_call x1, Pallas kernels, _suffix(): pl.pallas_call(_suffix_kernel, in_specs=[pl.BlockSpec(memory_space=pltpu....  5.47 us
    ppermute x3, starting transfers between devices, per_device(): lax.ppermute(pair, 'wide', [((i + 4 * d) % n_wide, i) for i in range(n_wi...  5.37 us
    pallas_call x1, Pallas kernels, _project(): pl.pallas_call(_project_kernel, grid=(parts,), in_specs=[whole((rows, 1))...  4.91 us
  transfers between devices with their start and end apart: 8, of which 4 were waited for; matrix products, arithmetic and copies ran while one was open for 3% of the time, Pallas kernels for 33%

profile of v2, /device:TPU:0, one launch (start us, length us, event | category | flops | bytes accessed | tf_op | source)
XLA Modules:
  0.0 111.6 jit_solution(6523901574850209010)
XLA Ops:
  0.0 1.7 %collective-permute-start = (bf16[64,1024]{1,0:T(8,128)(2,1)}, bf16[64,1024]{1,0:T(8,128)(2,1)S(1)}, u32[]{:S(2)}, u32[]{:S(2)}) collective-permute-start(bf16[64,1024]{1,0:T(8,128)(2,1)} %param.10), channel_id=1, source_target_pairs={{0,16},{8,24},{16,0},{24,8},{32,48},{40,56},{48,32},{56,40},{64,80... | collective-permute-start | bytes 393224 | tf_op jit(solution)/shard_map/ppermute | solution.py:648
  1.7 3.4 %copy.19 = bf16[4,128,8,256]{3,1,0,2:T(8,128)(2,1)} copy(bf16[4,128,8,256]{3,2,1,0:T(8,128)(2,1)} %param.15) | data formatting | bytes 4194304 | tf_op args[5]
  5.1 0.1 pad_add_fusion.place
  5.2 1.0 collective-permute-done
  6.1 7.1 %all-to-all-start = ((bf16[8,4,128,256]{3,2,1,0:T(8,128)(2,1)}), bf16[8,4,128,256]{3,2,1,0:T(8,128)(2,1)S(1)}, u32[]{:S(2)}, u32[]{:S(2)}) async-start(bf16[8,4,128,256]{3,2,1,0:T(8,128)(2,1)} %bitcast.23), calls=%async_computation | async-start | bytes 4194304 | tf_op jit(solution)/shard_map/all_to_all | solution.py:652
  13.3 4.1 %collective-permute-start.1 = (bf16[128,1024]{1,0:T(8,128)(2,1)S(1)}, bf16[128,1024]{1,0:T(8,128)(2,1)S(1)}, u32[]{:S(2)}, u32[]{:S(2)}) collective-permute-start(bf16[128,1024]{1,0:T(8,128)(2,1)S(1)} %maximum_select_fusion.refs_0_), channel_id=1, source_target_pairs={{32,0},{40,8},{48,16},{56,24},{64,32},{72,40},{80,48},{88,56},{96,... | collective-permute-start | bytes 786440 | tf_op jit(solution)/shard_map/ppermute | solution.py:661
  17.5 1.3 %collective-permute-start.3 = (bf16[128,1024]{1,0:T(8,128)(2,1)S(1)}, bf16[128,1024]{1,0:T(8,128)(2,1)S(1)}, u32[]{:S(2)}, u32[]{:S(2)}) collective-permute-start(bf16[128,1024]{1,0:T(8,128)(2,1)S(1)} %maximum_select_fusion.refs_0_), channel_id=1, source_target_pairs={{96,0},{104,8},{112,16},{120,24},{0,32},{8,40},{16,48},{24,56},{32... | collective-permute-start | bytes 786440 | tf_op jit(solution)/shard_map/ppermute | solution.py:661
  18.7 1.8 %keys.1 = (bf16[128,4096]{1,0:T(8,128)(2,1)S(1)}, bf16[4096,256]{1,0:T(8,128)(2,1)S(1)}) custom-call(bf16[2048,256]{1,0:T(8,128)(2,1)S(1)} %bitcast.18, bf16[2048,256]{1,0:T(8,128)(2,1)} %collective-permute-done.4.sib_ref), custom_call_target="tpu_custom_call" | custom-call | bytes 5242880 | tf_op jit(solution)/shard_map/keys/pallas_call | solution.py:58
  20.6 8.0 %system_attention.2 = (f32[128,1024]{1,0:T(8,128)}, f32[128,128]{1,0:T(8,128)}) custom-call(bf16[128,1024]{1,0:T(8,128)(2,1)} %copy-done.6, bf16[128,4096]{1,0:T(8,128)(2,1)S(1)} %get-tuple-element.36.refs_1_.refs_3_, bf16[4096,256]{1,0:T(8,128)(2,1)S(1)} %get-tuple-element.37.refs_2_.refs_4_), custom_call_target="tpu_custom_call" | custom-call | flops 3221225472 | bytes 3932160 | tf_op jit(solution)/shard_map/system_attention/pallas_call | solution.py:156
  28.6 3.0 %collective-permute-done.3.refs_2_.refs_3_ = bf16[128,1024]{1,0:T(8,128)(2,1)S(1)} collective-permute-done((bf16[128,1024]{1,0:T(8,128)(2,1)S(1)}, bf16[128,1024]{1,0:T(8,128)(2,1)S(1)}, u32[]{:S(2)}, u32[]{:S(2)}) %collective-permute-start.3) | collective-permute-done | bytes 262176 | tf_op jit(solution)/shard_map/ppermute | solution.py:661
  31.7 0.7 copy-done.9
  32.4 18.5 %system_attention.3 = (f32[128,1024]{1,0:T(8,128)}, f32[128,1024]{1,0:T(8,128)}, f32[128,1024]{1,0:T(8,128)}, f32[128,128]{1,0:T(8,128)}, f32[128,128]{1,0:T(8,128)}, /*index=5*/f32[128,128]{1,0:T(8,128)}) custom-call(bf16[128,1024]{1,0:T(8,128)(2,1)} %copy-done.7, bf16[128,1024]{1,0:T(8,128)(2,1)} %copy-done.8, bf16[128,1024]{1,0:T(8,128)(2,1)} %copy-done.9, ...), custom_call_target="tpu_custom_call" | custom-call | flops 9663676416 | bytes 5505024 | tf_op jit(solution)/shard_map/system_attention/pallas_call | solution.py:156
  50.9 0.1 collective-permute-start.5
  51.0 3.2 %plan.1 = (bf16[512,1024]{1,0:T(8,128)(2,1)S(1)}, bf16[512,512]{1,0:T(8,128)(2,1)S(1)}, s32[8,128]{1,0:T(8,128)S(1)}) custom-call(s32[2]{0:T(128)S(1)} %pad_add_fusion.place, s32[1,32]{1,0:T(1,128)S(1)} %bitcast.21, s32[8,128]{1,0:T(8,128)S(1)} %bitcast.20, bf16[128,1024]{1,0:T(8,128)(2,1)} %copy-done.6, bf16[128,1024]{1,0:T(8,128)(2,1)} %copy-done.7, ...), custom_call_target="tpu_custom_call" | custom-call | flops 536870912 | bytes 3145728 | tf_op jit(solution)/shard_map/plan/pallas_call | solution.py:282
  54.2 0.9 collective-permute-done.5.sib_ref
  55.2 8.8 %node_attention.1 = bf16[512,1152]{1,0:T(8,128)(2,1)} custom-call(s32[8,128]{1,0:T(8,128)S(1)} %get-tuple-element.47.table, s32[2]{0:T(128)S(1)} %pad_add_fusion.place, bf16[512,1024]{1,0:T(8,128)(2,1)S(1)} %get-tuple-element.48.qs, bf16[512,512]{1,0:T(8,128)(2,1)S(1)} %get-tuple-element.49.back_ref, bf16[32,128,256]{2,1,0:T(8,128)(2,1)S(1)} %bitcast.16, ...), custom_call_target="tpu_custom_call" | custom-call | flops 2000000000 | bytes 8388608 | tf_op jit(solution)/shard_map/node_attention/pallas_call | solution.py:409
  64.0 3.6 %all-to-all-start.1 = ((bf16[8,64,1152]{2,1,0:T(8,128)(2,1)}), bf16[8,64,1152]{2,1,0:T(8,128)(2,1)S(1)}, u32[]{:S(2)}, u32[]{:S(2)}) async-start(bf16[8,64,1152]{2,1,0:T(8,128)(2,1)} %bitcast.24), calls=%async_computation.1 | async-start | bytes 2359296 | tf_op jit(solution)/shard_map/all_to_all | solution.py:679
  67.5 0.1 dynamic-slice_bitcast_fusion
  67.6 0.1 copy.16.tenant_ref
  67.8 5.5 %suffix_attention.1 = (f32[64,8,128]{2,1,0:T(8,128)S(1)}, f32[64,8,128]{2,1,0:T(8,128)S(1)}) custom-call(s32[64]{0:T(128)S(1)} %copy-done.2, bf16[64,8,128]{2,1,0:T(8,128)(2,1)S(1)} %bitcast.19, bf16[64,256,256]{2,1,0:T(8,128)(2,1)} %bitcast.22), custom_call_target="tpu_custom_call" | custom-call | flops 1000000000 | bytes 8388608 | tf_op jit(solution)/shard_map/suffix_attention/pallas_call | solution.py:475
  73.2 12.0 %all-to-all-done.1.recv_ref = bf16[8,64,1152]{2,1,0:T(8,128)(2,1)S(1)} async-done(((bf16[8,64,1152]{2,1,0:T(8,128)(2,1)}), bf16[8,64,1152]{2,1,0:T(8,128)(2,1)S(1)}, u32[]{:S(2)}, u32[]{:S(2)}) %all-to-all-start.1) | async-done | bytes 1179680 | tf_op jit(solution)/shard_map/all_to_all | solution.py:679
  85.2 4.9 %project.1 = bf16[8,64,768]{2,1,0:T(8,128)(2,1)S(1)} custom-call(s32[64,1]{1,0:T(8,128)S(1)} %copy.16.tenant_ref, bf16[8,64,1152]{2,1,0:T(8,128)(2,1)S(1)} %all-to-all-done.1.recv_ref, f32[64,8,128]{2,1,0:T(8,128)S(1)} %get-tuple-element.59.o_ref, f32[64,8,128]{2,1,0:T(8,128)S(1)} %get-tuple-element.60.lse_ref, bf16[1024,5120]{1,0:T(8,128)(2,1)} %w_hbm.1, ...), custom_call_target="tpu_custom_call" | custom-call | flops 671088640 | bytes 10485760 | tf_op jit(solution)/shard_map/project/pallas_call | solution.py:566
  90.1 20.6 %all_to_all.15.recv_ref = bf16[8,64,768]{2,1,0:T(8,128)(2,1)S(1)} all-to-all(bf16[8,64,768]{2,1,0:T(8,128)(2,1)S(1)} %project.1), channel_id=1, replica_groups=mesh['wide'=16,'narrow'=8] {'narrow'}, dimensions={0} | all-to-all | bytes 1572864 | tf_op jit(solution)/shard_map/all_to_all | solution.py:697
  110.7 0.9 finish.1
  (27 shorter events, 0.1 us)
Async XLA Ops:
  0.0 18.7 %collective-permute-start.4 = (bf16[2048,256]{1,0:T(8,128)(2,1)}, bf16[2048,256]{1,0:T(8,128)(2,1)}, u32[]{:S(2)}, u32[]{:S(2)}) collective-permute-start(bf16[2048,256]{1,0:T(8,128)(2,1)} %bitcast.17), channel_id=1, source_target_pairs={{0,8},{8,0},{16,24},{24,16},{32,40},{40,32},{48,56},{56,48},{64,72... | collective-permute-start | bytes 3145736 | tf_op jit(solution)/shard_map/ppermute | solution.py:646
  0.0 6.1 %collective-permute-start = (bf16[64,1024]{1,0:T(8,128)(2,1)}, bf16[64,1024]{1,0:T(8,128)(2,1)S(1)}, u32[]{:S(2)}, u32[]{:S(2)}) collective-permute-start(bf16[64,1024]{1,0:T(8,128)(2,1)} %param.10), channel_id=1, source_target_pairs={{0,16},{8,24},{16,0},{24,8},{32,48},{40,56},{48,32},{56,40},{64,80... | collective-permute-start | bytes 393224 | tf_op jit(solution)/shard_map/ppermute | solution.py:648
  6.1 7.2 %copy-start.5 = (bf16[64,1024]{1,0:T(8,128)(2,1)S(1)}, bf16[64,1024]{1,0:T(8,128)(2,1)}, u32[]{:S(2)}) copy-start(bf16[64,1024]{1,0:T(8,128)(2,1)} %param.10) | copy-start | bytes 393220
  6.1 12.6 %copy-start = (bf16[2048,1,256]{2,0,1:T(8,128)(2,1)S(1)}, bf16[2048,1,256]{2,0,1:T(8,128)(2,1)}, u32[]{:S(2)}) copy-start(bf16[2048,1,256]{2,0,1:T(8,128)(2,1)} %param.14) | copy-start | bytes 3145732
  6.1 44.8 %all-to-all-start = ((bf16[8,4,128,256]{3,2,1,0:T(8,128)(2,1)}), bf16[8,4,128,256]{3,2,1,0:T(8,128)(2,1)S(1)}, u32[]{:S(2)}, u32[]{:S(2)}) async-start(bf16[8,4,128,256]{3,2,1,0:T(8,128)(2,1)} %bitcast.23), calls=%async_computation | async-start | bytes 4194304 | tf_op jit(solution)/shard_map/all_to_all | solution.py:652
  13.3 7.2 %copy-start.6 = (bf16[128,1024]{1,0:T(8,128)(2,1)}, bf16[128,1024]{1,0:T(8,128)(2,1)S(1)}, u32[]{:S(2)}) copy-start(bf16[128,1024]{1,0:T(8,128)(2,1)S(1)} %maximum_select_fusion.refs_0_) | copy-start | bytes 786436
  13.3 15.2 %collective-permute-start.1 = (bf16[128,1024]{1,0:T(8,128)(2,1)S(1)}, bf16[128,1024]{1,0:T(8,128)(2,1)S(1)}, u32[]{:S(2)}, u32[]{:S(2)}) collective-permute-start(bf16[128,1024]{1,0:T(8,128)(2,1)S(1)} %maximum_select_fusion.refs_0_), channel_id=1, source_target_pairs={{32,0},{40,8},{48,16},{56,24},{64,32},{72,40},{80,48},{88,56},{96,... | collective-permute-start | bytes 786440 | tf_op jit(solution)/shard_map/ppermute | solution.py:661
  17.5 11.2 %collective-permute-start.2 = (bf16[128,1024]{1,0:T(8,128)(2,1)S(1)}, bf16[128,1024]{1,0:T(8,128)(2,1)S(1)}, u32[]{:S(2)}, u32[]{:S(2)}) collective-permute-start(bf16[128,1024]{1,0:T(8,128)(2,1)S(1)} %maximum_select_fusion.refs_0_), channel_id=1, source_target_pairs={{64,0},{72,8},{80,16},{88,24},{96,32},{104,40},{112,48},{120,56},{... | collective-permute-start | bytes 786440 | tf_op jit(solution)/shard_map/ppermute | solution.py:661
  17.5 14.2 %collective-permute-start.3 = (bf16[128,1024]{1,0:T(8,128)(2,1)S(1)}, bf16[128,1024]{1,0:T(8,128)(2,1)S(1)}, u32[]{:S(2)}, u32[]{:S(2)}) collective-permute-start(bf16[128,1024]{1,0:T(8,128)(2,1)S(1)} %maximum_select_fusion.refs_0_), channel_id=1, source_target_pairs={{96,0},{104,8},{112,16},{120,24},{0,32},{8,40},{16,48},{24,56},{32... | collective-permute-start | bytes 786440 | tf_op jit(solution)/shard_map/ppermute | solution.py:661
  28.6 3.1 %copy-start.7 = (bf16[128,1024]{1,0:T(8,128)(2,1)}, bf16[128,1024]{1,0:T(8,128)(2,1)S(1)}, u32[]{:S(2)}) copy-start(bf16[128,1024]{1,0:T(8,128)(2,1)S(1)} %collective-permute-done.1.refs_0_.refs_1_) | copy-start | bytes 786436
  28.6 3.0 %copy-start.8 = (bf16[128,1024]{1,0:T(8,128)(2,1)}, bf16[128,1024]{1,0:T(8,128)(2,1)S(1)}, u32[]{:S(2)}) copy-start(bf16[128,1024]{1,0:T(8,128)(2,1)S(1)} %collective-permute-done.2.refs_1_.refs_2_) | copy-start | bytes 786436
  31.7 0.7 copy-start.9
  32.4 18.6 %copy-start.3 = (s32[1024]{0:T(1024)S(1)}, s32[1024]{0:T(1024)}, u32[]{:S(2)}) copy-start(s32[1024]{0:T(1024)} %param.11) | copy-start | bytes 12292
  32.4 18.6 %copy-start.4 = (s32[32]{0:T(128)S(1)}, s32[32]{0:T(128)}, u32[]{:S(2)}) copy-start(s32[32]{0:T(128)} %param.12) | copy-start | bytes 388
  50.9 4.2 %collective-permute-start.5 = (bf16[32,128,256]{2,1,0:T(8,128)(2,1)S(1)}, bf16[32,128,256]{2,1,0:T(8,128)(2,1)S(1)}, u32[]{:S(2)}, u32[]{:S(2)}) collective-permute-start(bf16[32,128,256]{2,1,0:T(8,128)(2,1)S(1)} %bitcast.15), channel_id=1, source_target_pairs={{0,8},{8,0},{16,24},{24,16},{32,40},{40,32},{48,56},{56,48},{64,72... | collective-permute-start | bytes 6291464 | tf_op jit(solution)/shard_map/ppermute | solution.py:672
  63.9 3.8 %copy-start.2 = (s32[64]{0:T(128)S(1)}, s32[64]{0:T(128)}, u32[]{:S(2)}) copy-start(s32[64]{0:T(128)} %len_ref.1) | copy-start | bytes 772
  64.0 21.3 %all-to-all-start.1 = ((bf16[8,64,1152]{2,1,0:T(8,128)(2,1)}), bf16[8,64,1152]{2,1,0:T(8,128)(2,1)S(1)}, u32[]{:S(2)}, u32[]{:S(2)}) async-start(bf16[8,64,1152]{2,1,0:T(8,128)(2,1)} %bitcast.24), calls=%async_computation.1 | async-start | bytes 2359296 | tf_op jit(solution)/shard_map/all_to_all | solution.py:679
  85.2 25.5 %copy-start.1 = (bf16[512,640]{1,0:T(8,128)(2,1)S(1)}, bf16[512,640]{1,0:T(8,128)(2,1)}, u32[]{:S(2)}) copy-start(bf16[512,640]{1,0:T(8,128)(2,1)} %up_ref.1) | copy-start | bytes 1966084

commit v3 on v2

--- a/solution.py
+++ b/solution.py
@@ -14,8 +14,8 @@
 BF16 = jnp.bfloat16
 SCALE2 = HEAD**-0.5 * 1.4426950408889634
 FLOOR = -1e30
-KEY_BLOCK = 2048
-HEADS_AT_ONCE = 2
+KEY_BLOCK = 512
+ONES = 16
 VISIT_ROWS = 16
 VISIT_UNROLL = 16
 
@@ -43,13 +43,13 @@
     return jnp.dot(a, b, preferred_element_type=F32)
 
 
-def _keys_kernel(own_ref, sib_ref, kt_ref, ve_ref):
+def _keys_kernel(own_ref, sib_ref, k_ref, vt_ref):
     n = own_ref.shape[0]
     for i, ref in enumerate((own_ref, sib_ref)):
         at = slice(i * n, (i + 1) * n)
-        kt_ref[:, at] = ref[:, :HEAD].T
-        ve_ref[at, :HEAD] = ref[:, HEAD:]
-        ve_ref[at, HEAD:] = jnp.ones((n, HEAD), BF16)
+        k_ref[at, :] = ref[:, :HEAD]
+        vt_ref[:HEAD, at] = ref[:, HEAD:].T
+    vt_ref[HEAD:, :] = jnp.ones((ONES, 2 * n), BF16)
 
 
 def _keys(own, sib):
@@ -60,97 +60,77 @@
         in_specs=[vmem] * 2,
         out_specs=[vmem] * 2,
         out_shape=[
-            pltpu.VMEM((HEAD, n), BF16),
-            pltpu.VMEM((n, 2 * HEAD), BF16),
+            pltpu.VMEM((n, HEAD), BF16),
+            pltpu.VMEM((HEAD + ONES, n), BF16),
         ],
         compiler_params=_params(16, False),
         cost_estimate=pl.CostEstimate(
-            flops=0, bytes_accessed=10 * n * HEAD, transcendentals=0
+            flops=0, bytes_accessed=8 * n * HEAD, transcendentals=0
         ),
         name="keys",
     )(own, sib)
 
 
 def _system_kernel(count, *refs):
-    q_hbm, (kt, ve) = refs[:count], refs[count : count + 2]
+    q_hbm, (k_ref, vt_ref) = refs[:count], refs[count : count + 2]
     o_hbm, lse_hbm = refs[count + 2 : 2 * count + 2], refs[2 * count + 2 : 3 * count + 2]
-    q_buf, o_buf, lse_buf, sems = refs[3 * count + 2 :]
-    steps = GROUP // HEADS_AT_ONCE
-    rows, keys = q_buf.shape[1], kt.shape[1]
+    q_buf, qt, o_buf, lse_buf, sems = refs[3 * count + 2 :]
+    rows, keys = q_buf.shape[1], k_ref.shape[0]
+    heads = [slice(g * HEAD, (g + 1) * HEAD) for g in range(GROUP)]
+    across = [slice(g * rows, (g + 1) * rows) for g in range(GROUP)]
     first = [
-        pltpu.make_async_copy(q_hbm[b], q_buf.at[b], sems.at[b, steps])
+        pltpu.make_async_copy(q_hbm[b], q_buf.at[b], sems.at[b, 0])
         for b in range(count)
     ]
     for copy in first:
         copy.start()
-    lane = _lane((rows, HEAD))
-    items = [
-        (h, b, k)
-        for h in range(HEADS_AT_ONCE)
-        for b in range(count)
-        for k in range(0, keys, KEY_BLOCK)
-    ]
     for b in range(count):
-        lse_buf[b] = jnp.zeros((rows, HEAD), F32)
-    for copy in first:
+        first[b].wait()
+        for g in range(GROUP):
+            qt[b, :, across[g]] = q_buf[b, :, heads[g]].T
+    items = [(b, k) for b in range(count) for k in range(0, keys, KEY_BLOCK)]
+
+    def score(item):
+        b, k = item
+        return _dot(k_ref[k : k + KEY_BLOCK, :], qt[b])
+
+    last = []
+    top = total = None
+    ahead = score(items[0])
+    for i, (b, k) in enumerate(items):
+        s = ahead
+        if i + 1 < len(items):
+            ahead = score(items[i + 1])
+        high = jnp.max(s, axis=0, keepdims=True) * SCALE2
+        if k:
+            high = jnp.maximum(high, top)
+        p = jnp.exp2(s * SCALE2 - high).astype(BF16)
+        r = _dot(vt_ref[:, k : k + KEY_BLOCK], p)
+        total = total * jnp.exp2(top - high) + r if k else r
+        top = high
+        if k + KEY_BLOCK < keys:
+            continue
+        l = total[HEAD : HEAD + 1, :]
+        o = total[:HEAD, :] / l
+        lse = top + jnp.log2(l)
+        for g in range(GROUP):
+            o_buf[b, :, heads[g]] = o[:, across[g]].T
+        lse = jnp.concatenate(
+            [lse[:, across[g]] for g in range(GROUP)]
+            + [jnp.zeros((HEAD - GROUP, rows), F32)],
+            axis=0,
+        )
+        lse_buf[b] = lse.T
+        for j, (src, dst) in enumerate([(o_buf, o_hbm), (lse_buf, lse_hbm)]):
+            copy = pltpu.make_async_copy(src.at[b], dst[b], sems.at[b, 1 + j])
+            copy.start()
+            last.append(copy)
+    for copy in last:
         copy.wait()
 
-    def send(b, step):
-        width = HEADS_AT_ONCE * HEAD
-        at = pl.ds(pl.multiple_of(step * width, width), width)
-        return pltpu.make_async_copy(
-            o_buf.at[b, :, at], o_hbm[b].at[:, at], sems.at[b, step]
-        )
-
-    def some_heads(step, carry):
-        def columns(h):
-            at = pl.multiple_of((step * HEADS_AT_ONCE + h) * HEAD, HEAD)
-            return pl.ds(at, HEAD)
-
-        def score(item):
-            h, b, k = item
-            return _dot(q_buf[b, :, columns(h)], kt[:, k : k + KEY_BLOCK])
-
-        top, total = {}, {}
-        ahead = score(items[0])
-        for i, (h, b, k) in enumerate(items):
-            s = ahead
-            if i + 1 < len(items):
-                ahead = score(items[i + 1])
-            high = jnp.max(s, axis=1, keepdims=True) * SCALE2
-            if (h, b) in top:
-                high = jnp.maximum(high, top[h, b])
-            p = jnp.exp2(s * SCALE2 - high).astype(BF16)
-            r = _dot(p, ve[k : k + KEY_BLOCK, :])
-            if (h, b) in top:
-                r = total[h, b] * jnp.exp2(top[h, b] - high) + r
-            top[h, b], total[h, b] = high, r
-        for b in range(count):
-            packed = lse_buf[b]
-            for h in range(HEADS_AT_ONCE):
-                l = total[h, b][:, HEAD:]
-                o_buf[b, :, columns(h)] = total[h, b][:, :HEAD] / l
-                lse = top[h, b] + jnp.log2(l)
-                packed = jnp.where(lane == step * HEADS_AT_ONCE + h, lse, packed)
-            lse_buf[b] = packed
-            send(b, step).start()
-        return carry
-
-    lax.fori_loop(0, steps, some_heads, 0)
-    last = [
-        pltpu.make_async_copy(lse_buf.at[b], lse_hbm[b], sems.at[b, steps])
-        for b in range(count)
-    ]
-    for copy in last:
-        copy.start()
-    for b in range(count):
-        for step in range(steps):
-            send(b, step).wait()
-        last[b].wait()
-
-
-def _system(qs, kt, ve):
-    count, rows, keys = len(qs), qs[0].shape[0], ve.shape[0]
+
+def _system(qs, k, vt):
+    count, rows, keys = len(qs), qs[0].shape[0], k.shape[0]
     vmem = pl.BlockSpec(memory_space=pltpu.VMEM)
     hbm = pl.BlockSpec(memory_space=pltpu.HBM)
     outs = pl.pallas_call(
@@ -161,18 +141,19 @@
         + [pltpu.HBM((rows, HEAD), F32)] * count,
         scratch_shapes=[
             pltpu.VMEM((count, rows, GROUP * HEAD), BF16),
+            pltpu.VMEM((count, HEAD, GROUP * rows), BF16),
             pltpu.VMEM((count, rows, GROUP * HEAD), F32),
             pltpu.VMEM((count, rows, HEAD), F32),
-            pltpu.SemaphoreType.DMA((count, GROUP // HEADS_AT_ONCE + 1)),
-        ],
-        compiler_params=_params(24, False),
+            pltpu.SemaphoreType.DMA((count, 3)),
+        ],
+        compiler_params=_params(40, False),
         cost_estimate=pl.CostEstimate(
             flops=6 * count * rows * GROUP * keys * HEAD,
             bytes_accessed=count * rows * 6 * GROUP * HEAD + 6 * keys * HEAD,
             transcendentals=count * rows * GROUP * keys,
         ),
         name="system_attention",
-    )(*map(_in_hbm, qs), *map(_in_vmem, [kt, ve]))
+    )(*map(_in_hbm, qs), *map(_in_vmem, [k, vt]))
     return list(outs[:count]), list(outs[count:])
 
 
@@ -661,10 +642,10 @@
         lax.ppermute(pair, "wide", [((i + 4 * d) % n_wide, i) for i in range(n_wide)])
         for d in range(1, layers)
     ]
-    kt, ve = _keys(own, sib)
-    o_a, lse_a = _system(pieces[:1], kt, ve)
+    keys, values = _keys(own, sib)
+    o_a, lse_a = _system(pieces[:1], keys, values)
     *pieces[1:], lse_a[0] = lax.optimization_barrier((*pieces[1:], lse_a[0]))
-    o_b, lse_b = _system(pieces[1:], kt, ve)
+    o_b, lse_b = _system(pieces[1:], keys, values)
     o_sys, lse_sys = [*o_a, *o_b], [*lse_a, *lse_b]
     nodes, lse_sys[-1], *pieces = lax.optimization_barrier(
         (nodes, lse_sys[-1], *pieces)

time: 112 us -> 112 us (level)
  Pallas kernels: 51.6 us -> 50.4 us
    pallas_call x2, Pallas kernels: 26.5 us -> 25.3 us  [_system(): pl.pallas_call(functools.partial(_system_kernel, count), in_specs=[hbm] *...]
  transfers between devices with their start and end apart: 8 -> 8, of which waited for: 4 -> 5; matrix products, arithmetic and copies ran while one was open for 3% -> 3% of each run, Pallas kernels for 33% -> 32%
where the time goes in v3:
time: 112 us; the launch traced here: 111 us
  Pallas kernels  50.4 us (45%)
  blocking collectives  20.6 us (18%)
  starting transfers between devices  17.8 us (16%)
  waiting for transfers between devices  17.8 us (16%)
  local copies, waits for them, and re-layouts  4.37 us (4%)
    pallas_call x2, Pallas kernels, _system(): pl.pallas_call(functools.partial(_system_kernel, count), in_specs=[hbm] *...  25.3 us
    all_to_all x1, blocking collectives, per_device(): parts = lax.all_to_all(parts, 'narrow', 0, 0, tiled=True)  20.6 us
    all_to_all x1, waiting for transfers between devices, per_device(): lax.all_to_all(sent.reshape(chips, rows, -1), 'wide', 0, 0, axis_index_gr...  12 us
    pallas_call x1, Pallas kernels, _node(): pl.pallas_call(functools.partial(_node_kernel, count), in_specs=[smem] *...  8.86 us
    all_to_all x1, starting transfers between devices, per_device(): nodes = lax.all_to_all(by_head, 'narrow', 0, 0, tiled=True)  7.15 us
    pallas_call x1, Pallas kernels, _suffix(): pl.pallas_call(_suffix_kernel, in_specs=[pl.BlockSpec(memory_space=pltpu....  5.47 us
    ppermute x3, starting transfers between devices, per_device(): lax.ppermute(pair, 'wide', [((i + 4 * d) % n_wide, i) for i in range(n_wi...  5.37 us
    pallas_call x1, Pallas kernels, _project(): pl.pallas_call(_project_kernel, grid=(parts,), in_specs=[whole((rows, 1))...  4.9 us
  transfers between devices with their start and end apart: 8, of which 5 were waited for; matrix products, arithmetic and copies ran while one was open for 3% of the time, Pallas kernels for 32%

profile of v3, /device:TPU:0, one launch (start us, length us, event | category | flops | bytes accessed | tf_op | source)
XLA Modules:
  0.0 111.3 jit_solution(1100304460497307653)
XLA Ops:
  0.0 1.7 %collective-permute-start = (bf16[64,1024]{1,0:T(8,128)(2,1)}, bf16[64,1024]{1,0:T(8,128)(2,1)S(1)}, u32[]{:S(2)}, u32[]{:S(2)}) collective-permute-start(bf16[64,1024]{1,0:T(8,128)(2,1)} %param.10), channel_id=1, source_target_pairs={{0,16},{8,24},{16,0},{24,8},{32,48},{40,56},{48,32},{56,40},{64,80... | collective-permute-start | bytes 393224 | tf_op jit(solution)/shard_map/ppermute | solution.py:629
  1.7 3.4 %copy.19 = bf16[4,128,8,256]{3,1,0,2:T(8,128)(2,1)} copy(bf16[4,128,8,256]{3,2,1,0:T(8,128)(2,1)} %param.15) | data formatting | bytes 4194304 | tf_op args[5]
  5.2 1.0 collective-permute-done
  6.1 7.1 %all-to-all-start = ((bf16[8,4,128,256]{3,2,1,0:T(8,128)(2,1)}), bf16[8,4,128,256]{3,2,1,0:T(8,128)(2,1)S(1)}, u32[]{:S(2)}, u32[]{:S(2)}) async-start(bf16[8,4,128,256]{3,2,1,0:T(8,128)(2,1)} %bitcast.23), calls=%async_computation | async-start | bytes 4194304 | tf_op jit(solution)/shard_map/all_to_all | solution.py:633
  13.3 4.1 %collective-permute-start.1 = (bf16[128,1024]{1,0:T(8,128)(2,1)S(1)}, bf16[128,1024]{1,0:T(8,128)(2,1)S(1)}, u32[]{:S(2)}, u32[]{:S(2)}) collective-permute-start(bf16[128,1024]{1,0:T(8,128)(2,1)S(1)} %maximum_select_fusion.refs_0_), channel_id=1, source_target_pairs={{32,0},{40,8},{48,16},{56,24},{64,32},{72,40},{80,48},{88,56},{96,... | collective-permute-start | bytes 786440 | tf_op jit(solution)/shard_map/ppermute | solution.py:642
  17.5 1.3 %collective-permute-start.3 = (bf16[128,1024]{1,0:T(8,128)(2,1)S(1)}, bf16[128,1024]{1,0:T(8,128)(2,1)S(1)}, u32[]{:S(2)}, u32[]{:S(2)}) collective-permute-start(bf16[128,1024]{1,0:T(8,128)(2,1)S(1)} %maximum_select_fusion.refs_0_), channel_id=1, source_target_pairs={{96,0},{104,8},{112,16},{120,24},{0,32},{8,40},{16,48},{24,56},{32... | collective-permute-start | bytes 786440 | tf_op jit(solution)/shard_map/ppermute | solution.py:642
  18.7 1.7 %keys.1 = (bf16[4096,128]{1,0:T(8,128)(2,1)S(1)}, bf16[144,4096]{1,0:T(8,128)(2,1)S(1)}) custom-call(bf16[2048,256]{1,0:T(8,128)(2,1)S(1)} %bitcast.18, bf16[2048,256]{1,0:T(8,128)(2,1)} %collective-permute-done.4.sib_ref), custom_call_target="tpu_custom_call" | custom-call | bytes 4194304 | tf_op jit(solution)/shard_map/keys/pallas_call | solution.py:58
  20.5 7.2 %system_attention.2 = (f32[128,1024]{1,0:T(8,128)}, f32[128,128]{1,0:T(8,128)}) custom-call(bf16[128,1024]{1,0:T(8,128)(2,1)} %copy-done.6, bf16[4096,128]{1,0:T(8,128)(2,1)S(1)} %get-tuple-element.36.refs_1_.refs_3_, bf16[144,4096]{1,0:T(8,128)(2,1)S(1)} %get-tuple-element.37.refs_2_.refs_4_), custom_call_target="tpu_custom_call" | custom-call | flops 3221225472 | bytes 3932160 | tf_op jit(solution)/shard_map/system_attention/pallas_call | solution.py:136
  27.7 0.5 collective-permute-done.1.refs_0_.refs_1_
  28.3 3.4 %collective-permute-done.3.refs_2_.refs_3_ = bf16[128,1024]{1,0:T(8,128)(2,1)S(1)} collective-permute-done((bf16[128,1024]{1,0:T(8,128)(2,1)S(1)}, bf16[128,1024]{1,0:T(8,128)(2,1)S(1)}, u32[]{:S(2)}, u32[]{:S(2)}) %collective-permute-start.3) | collective-permute-done | bytes 262176 | tf_op jit(solution)/shard_map/ppermute | solution.py:642
  31.7 0.7 copy-done.9
  32.4 18.1 %system_attention.3 = (f32[128,1024]{1,0:T(8,128)}, f32[128,1024]{1,0:T(8,128)}, f32[128,1024]{1,0:T(8,128)}, f32[128,128]{1,0:T(8,128)}, f32[128,128]{1,0:T(8,128)}, /*index=5*/f32[128,128]{1,0:T(8,128)}) custom-call(bf16[128,1024]{1,0:T(8,128)(2,1)} %copy-done.7, bf16[128,1024]{1,0:T(8,128)(2,1)} %copy-done.8, bf16[128,1024]{1,0:T(8,128)(2,1)} %copy-done.9, ...), custom_call_target="tpu_custom_call" | custom-call | flops 9663676416 | bytes 5505024 | tf_op jit(solution)/shard_map/system_attention/pallas_call | solution.py:136
  50.5 0.1 collective-permute-start.5
  50.6 3.2 %plan.1 = (bf16[512,1024]{1,0:T(8,128)(2,1)S(1)}, bf16[512,512]{1,0:T(8,128)(2,1)S(1)}, s32[8,128]{1,0:T(8,128)S(1)}) custom-call(s32[2]{0:T(128)S(1)} %pad_add_fusion.place, s32[1,32]{1,0:T(1,128)S(1)} %bitcast.21, s32[8,128]{1,0:T(8,128)S(1)} %bitcast.20, bf16[128,1024]{1,0:T(8,128)(2,1)} %copy-done.6, bf16[128,1024]{1,0:T(8,128)(2,1)} %copy-done.7, ...), custom_call_target="tpu_custom_call" | custom-call | flops 536870912 | bytes 3145728 | tf_op jit(solution)/shard_map/plan/pallas_call | solution.py:263
  53.8 0.9 collective-permute-done.5.sib_ref
  54.7 8.9 %node_attention.1 = bf16[512,1152]{1,0:T(8,128)(2,1)} custom-call(s32[8,128]{1,0:T(8,128)S(1)} %get-tuple-element.47.table, s32[2]{0:T(128)S(1)} %pad_add_fusion.place, bf16[512,1024]{1,0:T(8,128)(2,1)S(1)} %get-tuple-element.48.qs, bf16[512,512]{1,0:T(8,128)(2,1)S(1)} %get-tuple-element.49.back_ref, bf16[32,128,256]{2,1,0:T(8,128)(2,1)S(1)} %bitcast.16, ...), custom_call_target="tpu_custom_call" | custom-call | flops 2000000000 | bytes 8388608 | tf_op jit(solution)/shard_map/node_attention/pallas_call | solution.py:390
  63.6 3.6 %all-to-all-start.1 = ((bf16[8,64,1152]{2,1,0:T(8,128)(2,1)}), bf16[8,64,1152]{2,1,0:T(8,128)(2,1)S(1)}, u32[]{:S(2)}, u32[]{:S(2)}) async-start(bf16[8,64,1152]{2,1,0:T(8,128)(2,1)} %bitcast.24), calls=%async_computation.1 | async-start | bytes 2359296 | tf_op jit(solution)/shard_map/all_to_all | solution.py:660
  67.2 0.1 dynamic-slice_bitcast_fusion
  67.3 0.1 copy.16.tenant_ref
  67.4 5.5 %suffix_attention.1 = (f32[64,8,128]{2,1,0:T(8,128)S(1)}, f32[64,8,128]{2,1,0:T(8,128)S(1)}) custom-call(s32[64]{0:T(128)S(1)} %copy-done.2, bf16[64,8,128]{2,1,0:T(8,128)(2,1)S(1)} %bitcast.19, bf16[64,256,256]{2,1,0:T(8,128)(2,1)} %bitcast.22), custom_call_target="tpu_custom_call" | custom-call | flops 1000000000 | bytes 8388608 | tf_op jit(solution)/shard_map/suffix_attention/pallas_call | solution.py:456
  72.9 12.0 %all-to-all-done.1.recv_ref = bf16[8,64,1152]{2,1,0:T(8,128)(2,1)S(1)} async-done(((bf16[8,64,1152]{2,1,0:T(8,128)(2,1)}), bf16[8,64,1152]{2,1,0:T(8,128)(2,1)S(1)}, u32[]{:S(2)}, u32[]{:S(2)}) %all-to-all-start.1) | async-done | bytes 1179680 | tf_op jit(solution)/shard_map/all_to_all | solution.py:660
  84.8 4.9 %project.1 = bf16[8,64,768]{2,1,0:T(8,128)(2,1)S(1)} custom-call(s32[64,1]{1,0:T(8,128)S(1)} %copy.16.tenant_ref, bf16[8,64,1152]{2,1,0:T(8,128)(2,1)S(1)} %all-to-all-done.1.recv_ref, f32[64,8,128]{2,1,0:T(8,128)S(1)} %get-tuple-element.59.o_ref, f32[64,8,128]{2,1,0:T(8,128)S(1)} %get-tuple-element.60.lse_ref, bf16[1024,5120]{1,0:T(8,128)(2,1)} %w_hbm.1, ...), custom_call_target="tpu_custom_call" | custom-call | flops 671088640 | bytes 10485760 | tf_op jit(solution)/shard_map/project/pallas_call | solution.py:547
  89.8 20.6 %all_to_all.15.recv_ref = bf16[8,64,768]{2,1,0:T(8,128)(2,1)S(1)} all-to-all(bf16[8,64,768]{2,1,0:T(8,128)(2,1)S(1)} %project.1), channel_id=1, replica_groups=mesh['wide'=16,'narrow'=8] {'narrow'}, dimensions={0} | all-to-all | bytes 1572864 | tf_op jit(solution)/shard_map/all_to_all | solution.py:678
  110.4 0.9 finish.1
  (27 shorter events, 0.2 us)
Async XLA Ops:
  0.0 18.7 %collective-permute-start.4 = (bf16[2048,256]{1,0:T(8,128)(2,1)}, bf16[2048,256]{1,0:T(8,128)(2,1)}, u32[]{:S(2)}, u32[]{:S(2)}) collective-permute-start(bf16[2048,256]{1,0:T(8,128)(2,1)} %bitcast.17), channel_id=1, source_target_pairs={{0,8},{8,0},{16,24},{24,16},{32,40},{40,32},{48,56},{56,48},{64,72... | collective-permute-start | bytes 3145736 | tf_op jit(solution)/shard_map/ppermute | solution.py:627
  0.0 6.1 %collective-permute-start = (bf16[64,1024]{1,0:T(8,128)(2,1)}, bf16[64,1024]{1,0:T(8,128)(2,1)S(1)}, u32[]{:S(2)}, u32[]{:S(2)}) collective-permute-start(bf16[64,1024]{1,0:T(8,128)(2,1)} %param.10), channel_id=1, source_target_pairs={{0,16},{8,24},{16,0},{24,8},{32,48},{40,56},{48,32},{56,40},{64,80... | collective-permute-start | bytes 393224 | tf_op jit(solution)/shard_map/ppermute | solution.py:629
  6.1 7.2 %copy-start.5 = (bf16[64,1024]{1,0:T(8,128)(2,1)S(1)}, bf16[64,1024]{1,0:T(8,128)(2,1)}, u32[]{:S(2)}) copy-start(bf16[64,1024]{1,0:T(8,128)(2,1)} %param.10) | copy-start | bytes 393220
  6.1 12.6 %copy-start = (bf16[2048,1,256]{2,0,1:T(8,128)(2,1)S(1)}, bf16[2048,1,256]{2,0,1:T(8,128)(2,1)}, u32[]{:S(2)}) copy-start(bf16[2048,1,256]{2,0,1:T(8,128)(2,1)} %param.14) | copy-start | bytes 3145732
  6.1 44.3 %all-to-all-start = ((bf16[8,4,128,256]{3,2,1,0:T(8,128)(2,1)}), bf16[8,4,128,256]{3,2,1,0:T(8,128)(2,1)S(1)}, u32[]{:S(2)}, u32[]{:S(2)}) async-start(bf16[8,4,128,256]{3,2,1,0:T(8,128)(2,1)} %bitcast.23), calls=%async_computation | async-start | bytes 4194304 | tf_op jit(solution)/shard_map/all_to_all | solution.py:633
  13.3 7.1 %copy-start.6 = (bf16[128,1024]{1,0:T(8,128)(2,1)}, bf16[128,1024]{1,0:T(8,128)(2,1)S(1)}, u32[]{:S(2)}) copy-start(bf16[128,1024]{1,0:T(8,128)(2,1)S(1)} %maximum_select_fusion.refs_0_) | copy-start | bytes 786436
  13.3 14.9 %collective-permute-start.1 = (bf16[128,1024]{1,0:T(8,128)(2,1)S(1)}, bf16[128,1024]{1,0:T(8,128)(2,1)S(1)}, u32[]{:S(2)}, u32[]{:S(2)}) collective-permute-start(bf16[128,1024]{1,0:T(8,128)(2,1)S(1)} %maximum_select_fusion.refs_0_), channel_id=1, source_target_pairs={{32,0},{40,8},{48,16},{56,24},{64,32},{72,40},{80,48},{88,56},{96,... | collective-permute-start | bytes 786440 | tf_op jit(solution)/shard_map/ppermute | solution.py:642
  17.5 10.8 %collective-permute-start.2 = (bf16[128,1024]{1,0:T(8,128)(2,1)S(1)}, bf16[128,1024]{1,0:T(8,128)(2,1)S(1)}, u32[]{:S(2)}, u32[]{:S(2)}) collective-permute-start(bf16[128,1024]{1,0:T(8,128)(2,1)S(1)} %maximum_select_fusion.refs_0_), channel_id=1, source_target_pairs={{64,0},{72,8},{80,16},{88,24},{96,32},{104,40},{112,48},{120,56},{... | collective-permute-start | bytes 786440 | tf_op jit(solution)/shard_map/ppermute | solution.py:642
  17.5 14.2 %collective-permute-start.3 = (bf16[128,1024]{1,0:T(8,128)(2,1)S(1)}, bf16[128,1024]{1,0:T(8,128)(2,1)S(1)}, u32[]{:S(2)}, u32[]{:S(2)}) collective-permute-start(bf16[128,1024]{1,0:T(8,128)(2,1)S(1)} %maximum_select_fusion.refs_0_), channel_id=1, source_target_pairs={{96,0},{104,8},{112,16},{120,24},{0,32},{8,40},{16,48},{24,56},{32... | collective-permute-start | bytes 786440 | tf_op jit(solution)/shard_map/ppermute | solution.py:642
  28.2 3.4 %copy-start.7 = (bf16[128,1024]{1,0:T(8,128)(2,1)}, bf16[128,1024]{1,0:T(8,128)(2,1)S(1)}, u32[]{:S(2)}) copy-start(bf16[128,1024]{1,0:T(8,128)(2,1)S(1)} %collective-permute-done.1.refs_0_.refs_1_) | copy-start | bytes 786436
  28.3 3.4 %copy-start.8 = (bf16[128,1024]{1,0:T(8,128)(2,1)}, bf16[128,1024]{1,0:T(8,128)(2,1)S(1)}, u32[]{:S(2)}) copy-start(bf16[128,1024]{1,0:T(8,128)(2,1)S(1)} %collective-permute-done.2.refs_1_.refs_2_) | copy-start | bytes 786436
  31.7 0.7 copy-start.9
  32.4 18.2 %copy-start.3 = (s32[1024]{0:T(1024)S(1)}, s32[1024]{0:T(1024)}, u32[]{:S(2)}) copy-start(s32[1024]{0:T(1024)} %param.11) | copy-start | bytes 12292
  32.4 18.2 %copy-start.4 = (s32[32]{0:T(128)S(1)}, s32[32]{0:T(128)}, u32[]{:S(2)}) copy-start(s32[32]{0:T(128)} %param.12) | copy-start | bytes 388
  50.5 4.2 %collective-permute-start.5 = (bf16[32,128,256]{2,1,0:T(8,128)(2,1)S(1)}, bf16[32,128,256]{2,1,0:T(8,128)(2,1)S(1)}, u32[]{:S(2)}, u32[]{:S(2)}) collective-permute-start(bf16[32,128,256]{2,1,0:T(8,128)(2,1)S(1)} %bitcast.15), channel_id=1, source_target_pairs={{0,8},{8,0},{16,24},{24,16},{32,40},{40,32},{48,56},{56,48},{64,72... | collective-permute-start | bytes 6291464 | tf_op jit(solution)/shard_map/ppermute | solution.py:653
  63.6 3.8 %copy-start.2 = (s32[64]{0:T(128)S(1)}, s32[64]{0:T(128)}, u32[]{:S(2)}) copy-start(s32[64]{0:T(128)} %len_ref.1) | copy-start | bytes 772
  63.6 21.3 %all-to-all-start.1 = ((bf16[8,64,1152]{2,1,0:T(8,128)(2,1)}), bf16[8,64,1152]{2,1,0:T(8,128)(2,1)S(1)}, u32[]{:S(2)}, u32[]{:S(2)}) async-start(bf16[8,64,1152]{2,1,0:T(8,128)(2,1)} %bitcast.24), calls=%async_computation.1 | async-start | bytes 2359296 | tf_op jit(solution)/shard_map/all_to_all | solution.py:660
  84.8 25.5 %copy-start.1 = (bf16[512,640]{1,0:T(8,128)(2,1)S(1)}, bf16[512,640]{1,0:T(8,128)(2,1)}, u32[]{:S(2)}) copy-start(bf16[512,640]{1,0:T(8,128)(2,1)} %up_ref.1) | copy-start | bytes 1966084

commit v4 on v3

--- a/solution.py
+++ b/solution.py
@@ -531,9 +531,11 @@
             kept = kept + reduced[:, c : c + HEAD]
         low[...] = kept.astype(BF16)
 
-    fetch_w(step).wait()
-    out_ref[0, :, :width] = _dot(att[...], w_ref[step]).astype(BF16)
-    out_ref[0, :, width:] = low[...]
+    for i in range(out_ref.shape[0]):
+        d = step * out_ref.shape[0] + i
+        fetch_w(d).wait()
+        out_ref[i, :, :width] = _dot(att[...], w_ref[d]).astype(BF16)
+        out_ref[i, :, width:] = low[...]
 
 
 def _project(tenant, recv, o, lse, weight, down, parts):
@@ -546,7 +548,7 @@
 
     return pl.pallas_call(
         _project_kernel,
-        grid=(parts,),
+        grid=(parts // 4,),
         in_specs=[
             whole((rows, 1)),
             whole(recv.shape),
@@ -555,7 +557,7 @@
             pl.BlockSpec(memory_space=pltpu.HBM),
             pl.BlockSpec(memory_space=pltpu.HBM),
         ],
-        out_specs=pl.BlockSpec((1, rows, width + HEAD), lambda d: (d, 0, 0)),
+        out_specs=pl.BlockSpec((4, rows, width + HEAD), lambda d: (d, 0, 0)),
         out_shape=jax.ShapeDtypeStruct((parts, rows, width + HEAD), BF16),
         scratch_shapes=[
             pltpu.VMEM((rows, GROUP * HEAD), BF16),

time: 112 us -> 112 us (level)
  no operation moved by 1% of the time
where the time goes in v4:
time: 112 us; the launch traced here: 111 us
  Pallas kernels  50.4 us (45%)
  blocking collectives  20.6 us (18%)
  starting transfers between devices  17.8 us (16%)
  waiting for transfers between devices  17.8 us (16%)
  local copies, waits for them, and re-layouts  4.37 us (4%)
    pallas_call x2, Pallas kernels, _system(): pl.pallas_call(functools.partial(_system_kernel, count), in_specs=[hbm] *...  25.3 us
    all_to_all x1, blocking collectives, per_device(): parts = lax.all_to_all(parts, 'narrow', 0, 0, tiled=True)  20.6 us
    all_to_all x1, waiting for transfers between devices, per_device(): lax.all_to_all(sent.reshape(chips, rows, -1), 'wide', 0, 0, axis_index_gr...  12 us
    pallas_call x1, Pallas kernels, _node(): pl.pallas_call(functools.partial(_node_kernel, count), in_specs=[smem] *...  8.86 us
    all_to_all x1, starting transfers between devices, per_device(): nodes = lax.all_to_all(by_head, 'narrow', 0, 0, tiled=True)  7.15 us
    pallas_call x1, Pallas kernels, _suffix(): pl.pallas_call(_suffix_kernel, in_specs=[pl.BlockSpec(memory_space=pltpu....  5.47 us
    ppermute x3, starting transfers between devices, per_device(): lax.ppermute(pair, 'wide', [((i + 4 * d) % n_wide, i) for i in range(n_wi...  5.37 us
    pallas_call x1, Pallas kernels, _project(): pl.pallas_call(_project_kernel, grid=(parts // 4,), in_specs=[whole((rows...  4.91 us
  transfers between devices with their start and end apart: 8, of which 5 were waited for; matrix products, arithmetic and copies ran while one was open for 3% of the time, Pallas kernels for 32%

profile of v4, /device:TPU:0, one launch (start us, length us, event | category | flops | bytes accessed | tf_op | source)
XLA Modules:
  0.0 111.3 jit_solution(14429363412249270724)
XLA Ops:
  0.0 1.7 %collective-permute-start = (bf16[64,1024]{1,0:T(8,128)(2,1)}, bf16[64,1024]{1,0:T(8,128)(2,1)S(1)}, u32[]{:S(2)}, u32[]{:S(2)}) collective-permute-start(bf16[64,1024]{1,0:T(8,128)(2,1)} %param.10), channel_id=1, source_target_pairs={{0,16},{8,24},{16,0},{24,8},{32,48},{40,56},{48,32},{56,40},{64,80... | collective-permute-start | bytes 393224 | tf_op jit(solution)/shard_map/ppermute | solution.py:631
  1.7 3.4 %copy.19 = bf16[4,128,8,256]{3,1,0,2:T(8,128)(2,1)} copy(bf16[4,128,8,256]{3,2,1,0:T(8,128)(2,1)} %param.15) | data formatting | bytes 4194304 | tf_op args[5]
  5.2 1.0 collective-permute-done
  6.1 7.1 %all-to-all-start = ((bf16[8,4,128,256]{3,2,1,0:T(8,128)(2,1)}), bf16[8,4,128,256]{3,2,1,0:T(8,128)(2,1)S(1)}, u32[]{:S(2)}, u32[]{:S(2)}) async-start(bf16[8,4,128,256]{3,2,1,0:T(8,128)(2,1)} %bitcast.23), calls=%async_computation | async-start | bytes 4194304 | tf_op jit(solution)/shard_map/all_to_all | solution.py:635
  13.3 4.1 %collective-permute-start.1 = (bf16[128,1024]{1,0:T(8,128)(2,1)S(1)}, bf16[128,1024]{1,0:T(8,128)(2,1)S(1)}, u32[]{:S(2)}, u32[]{:S(2)}) collective-permute-start(bf16[128,1024]{1,0:T(8,128)(2,1)S(1)} %maximum_select_fusion.refs_0_), channel_id=1, source_target_pairs={{32,0},{40,8},{48,16},{56,24},{64,32},{72,40},{80,48},{88,56},{96,... | collective-permute-start | bytes 786440 | tf_op jit(solution)/shard_map/ppermute | solution.py:644
  17.5 1.3 %collective-permute-start.3 = (bf16[128,1024]{1,0:T(8,128)(2,1)S(1)}, bf16[128,1024]{1,0:T(8,128)(2,1)S(1)}, u32[]{:S(2)}, u32[]{:S(2)}) collective-permute-start(bf16[128,1024]{1,0:T(8,128)(2,1)S(1)} %maximum_select_fusion.refs_0_), channel_id=1, source_target_pairs={{96,0},{104,8},{112,16},{120,24},{0,32},{8,40},{16,48},{24,56},{32... | collective-permute-start | bytes 786440 | tf_op jit(solution)/shard_map/ppermute | solution.py:644
  18.7 1.7 %keys.1 = (bf16[4096,128]{1,0:T(8,128)(2,1)S(1)}, bf16[144,4096]{1,0:T(8,128)(2,1)S(1)}) custom-call(bf16[2048,256]{1,0:T(8,128)(2,1)S(1)} %bitcast.18, bf16[2048,256]{1,0:T(8,128)(2,1)} %collective-permute-done.4.sib_ref), custom_call_target="tpu_custom_call" | custom-call | bytes 4194304 | tf_op jit(solution)/shard_map/keys/pallas_call | solution.py:58
  20.5 7.2 %system_attention.2 = (f32[128,1024]{1,0:T(8,128)}, f32[128,128]{1,0:T(8,128)}) custom-call(bf16[128,1024]{1,0:T(8,128)(2,1)} %copy-done.6, bf16[4096,128]{1,0:T(8,128)(2,1)S(1)} %get-tuple-element.36.refs_1_.refs_3_, bf16[144,4096]{1,0:T(8,128)(2,1)S(1)} %get-tuple-element.37.refs_2_.refs_4_), custom_call_target="tpu_custom_call" | custom-call | flops 3221225472 | bytes 3932160 | tf_op jit(solution)/shard_map/system_attention/pallas_call | solution.py:136
  27.7 0.5 collective-permute-done.1.refs_0_.refs_1_
  28.3 3.4 %collective-permute-done.3.refs_2_.refs_3_ = bf16[128,1024]{1,0:T(8,128)(2,1)S(1)} collective-permute-done((bf16[128,1024]{1,0:T(8,128)(2,1)S(1)}, bf16[128,1024]{1,0:T(8,128)(2,1)S(1)}, u32[]{:S(2)}, u32[]{:S(2)}) %collective-permute-start.3) | collective-permute-done | bytes 262176 | tf_op jit(solution)/shard_map/ppermute | solution.py:644
  31.7 0.7 copy-done.9
  32.4 18.1 %system_attention.3 = (f32[128,1024]{1,0:T(8,128)}, f32[128,1024]{1,0:T(8,128)}, f32[128,1024]{1,0:T(8,128)}, f32[128,128]{1,0:T(8,128)}, f32[128,128]{1,0:T(8,128)}, /*index=5*/f32[128,128]{1,0:T(8,128)}) custom-call(bf16[128,1024]{1,0:T(8,128)(2,1)} %copy-done.7, bf16[128,1024]{1,0:T(8,128)(2,1)} %copy-done.8, bf16[128,1024]{1,0:T(8,128)(2,1)} %copy-done.9, ...), custom_call_target="tpu_custom_call" | custom-call | flops 9663676416 | bytes 5505024 | tf_op jit(solution)/shard_map/system_attention/pallas_call | solution.py:136
  50.5 0.1 collective-permute-start.5
  50.6 3.2 %plan.1 = (bf16[512,1024]{1,0:T(8,128)(2,1)S(1)}, bf16[512,512]{1,0:T(8,128)(2,1)S(1)}, s32[8,128]{1,0:T(8,128)S(1)}) custom-call(s32[2]{0:T(128)S(1)} %pad_add_fusion.place, s32[1,32]{1,0:T(1,128)S(1)} %bitcast.21, s32[8,128]{1,0:T(8,128)S(1)} %bitcast.20, bf16[128,1024]{1,0:T(8,128)(2,1)} %copy-done.6, bf16[128,1024]{1,0:T(8,128)(2,1)} %copy-done.7, ...), custom_call_target="tpu_custom_call" | custom-call | flops 536870912 | bytes 3145728 | tf_op jit(solution)/shard_map/plan/pallas_call | solution.py:263
  53.8 0.9 collective-permute-done.5.sib_ref
  54.7 8.9 %node_attention.1 = bf16[512,1152]{1,0:T(8,128)(2,1)} custom-call(s32[8,128]{1,0:T(8,128)S(1)} %get-tuple-element.47.table, s32[2]{0:T(128)S(1)} %pad_add_fusion.place, bf16[512,1024]{1,0:T(8,128)(2,1)S(1)} %get-tuple-element.48.qs, bf16[512,512]{1,0:T(8,128)(2,1)S(1)} %get-tuple-element.49.back_ref, bf16[32,128,256]{2,1,0:T(8,128)(2,1)S(1)} %bitcast.16, ...), custom_call_target="tpu_custom_call" | custom-call | flops 2000000000 | bytes 8388608 | tf_op jit(solution)/shard_map/node_attention/pallas_call | solution.py:390
  63.6 3.6 %all-to-all-start.1 = ((bf16[8,64,1152]{2,1,0:T(8,128)(2,1)}), bf16[8,64,1152]{2,1,0:T(8,128)(2,1)S(1)}, u32[]{:S(2)}, u32[]{:S(2)}) async-start(bf16[8,64,1152]{2,1,0:T(8,128)(2,1)} %bitcast.24), calls=%async_computation.1 | async-start | bytes 2359296 | tf_op jit(solution)/shard_map/all_to_all | solution.py:662
  67.2 0.1 dynamic-slice_bitcast_fusion
  67.2 0.1 copy.16.tenant_ref
  67.4 5.5 %suffix_attention.1 = (f32[64,8,128]{2,1,0:T(8,128)S(1)}, f32[64,8,128]{2,1,0:T(8,128)S(1)}) custom-call(s32[64]{0:T(128)S(1)} %copy-done.2, bf16[64,8,128]{2,1,0:T(8,128)(2,1)S(1)} %bitcast.19, bf16[64,256,256]{2,1,0:T(8,128)(2,1)} %bitcast.22), custom_call_target="tpu_custom_call" | custom-call | flops 1000000000 | bytes 8388608 | tf_op jit(solution)/shard_map/suffix_attention/pallas_call | solution.py:456
  72.9 12.0 %all-to-all-done.1.recv_ref = bf16[8,64,1152]{2,1,0:T(8,128)(2,1)S(1)} async-done(((bf16[8,64,1152]{2,1,0:T(8,128)(2,1)}), bf16[8,64,1152]{2,1,0:T(8,128)(2,1)S(1)}, u32[]{:S(2)}, u32[]{:S(2)}) %all-to-all-start.1) | async-done | bytes 1179680 | tf_op jit(solution)/shard_map/all_to_all | solution.py:662
  84.8 4.9 %project.1 = bf16[8,64,768]{2,1,0:T(8,128)(2,1)S(1)} custom-call(s32[64,1]{1,0:T(8,128)S(1)} %copy.16.tenant_ref, bf16[8,64,1152]{2,1,0:T(8,128)(2,1)S(1)} %all-to-all-done.1.recv_ref, f32[64,8,128]{2,1,0:T(8,128)S(1)} %get-tuple-element.59.o_ref, f32[64,8,128]{2,1,0:T(8,128)S(1)} %get-tuple-element.60.lse_ref, bf16[1024,5120]{1,0:T(8,128)(2,1)} %w_hbm.1, ...), custom_call_target="tpu_custom_call" | custom-call | flops 671088640 | bytes 10485760 | tf_op jit(solution)/shard_map/project/pallas_call | solution.py:549
  89.8 20.6 %all_to_all.15.recv_ref = bf16[8,64,768]{2,1,0:T(8,128)(2,1)S(1)} all-to-all(bf16[8,64,768]{2,1,0:T(8,128)(2,1)S(1)} %project.1), channel_id=1, replica_groups=mesh['wide'=16,'narrow'=8] {'narrow'}, dimensions={0} | all-to-all | bytes 1572864 | tf_op jit(solution)/shard_map/all_to_all | solution.py:680
  110.4 0.9 finish.1
  (27 shorter events, 0.2 us)
Async XLA Ops:
  0.0 18.7 %collective-permute-start.4 = (bf16[2048,256]{1,0:T(8,128)(2,1)}, bf16[2048,256]{1,0:T(8,128)(2,1)}, u32[]{:S(2)}, u32[]{:S(2)}) collective-permute-start(bf16[2048,256]{1,0:T(8,128)(2,1)} %bitcast.17), channel_id=1, source_target_pairs={{0,8},{8,0},{16,24},{24,16},{32,40},{40,32},{48,56},{56,48},{64,72... | collective-permute-start | bytes 3145736 | tf_op jit(solution)/shard_map/ppermute | solution.py:629
  0.0 6.1 %collective-permute-start = (bf16[64,1024]{1,0:T(8,128)(2,1)}, bf16[64,1024]{1,0:T(8,128)(2,1)S(1)}, u32[]{:S(2)}, u32[]{:S(2)}) collective-permute-start(bf16[64,1024]{1,0:T(8,128)(2,1)} %param.10), channel_id=1, source_target_pairs={{0,16},{8,24},{16,0},{24,8},{32,48},{40,56},{48,32},{56,40},{64,80... | collective-permute-start | bytes 393224 | tf_op jit(solution)/shard_map/ppermute | solution.py:631
  6.1 7.2 %copy-start.5 = (bf16[64,1024]{1,0:T(8,128)(2,1)S(1)}, bf16[64,1024]{1,0:T(8,128)(2,1)}, u32[]{:S(2)}) copy-start(bf16[64,1024]{1,0:T(8,128)(2,1)} %param.10) | copy-start | bytes 393220
  6.1 12.6 %copy-start = (bf16[2048,1,256]{2,0,1:T(8,128)(2,1)S(1)}, bf16[2048,1,256]{2,0,1:T(8,128)(2,1)}, u32[]{:S(2)}) copy-start(bf16[2048,1,256]{2,0,1:T(8,128)(2,1)} %param.14) | copy-start | bytes 3145732
  6.1 44.3 %all-to-all-start = ((bf16[8,4,128,256]{3,2,1,0:T(8,128)(2,1)}), bf16[8,4,128,256]{3,2,1,0:T(8,128)(2,1)S(1)}, u32[]{:S(2)}, u32[]{:S(2)}) async-start(bf16[8,4,128,256]{3,2,1,0:T(8,128)(2,1)} %bitcast.23), calls=%async_computation | async-start | bytes 4194304 | tf_op jit(solution)/shard_map/all_to_all | solution.py:635
  13.3 7.1 %copy-start.6 = (bf16[128,1024]{1,0:T(8,128)(2,1)}, bf16[128,1024]{1,0:T(8,128)(2,1)S(1)}, u32[]{:S(2)}) copy-start(bf16[128,1024]{1,0:T(8,128)(2,1)S(1)} %maximum_select_fusion.refs_0_) | copy-start | bytes 786436
  13.3 14.9 %collective-permute-start.1 = (bf16[128,1024]{1,0:T(8,128)(2,1)S(1)}, bf16[128,1024]{1,0:T(8,128)(2,1)S(1)}, u32[]{:S(2)}, u32[]{:S(2)}) collective-permute-start(bf16[128,1024]{1,0:T(8,128)(2,1)S(1)} %maximum_select_fusion.refs_0_), channel_id=1, source_target_pairs={{32,0},{40,8},{48,16},{56,24},{64,32},{72,40},{80,48},{88,56},{96,... | collective-permute-start | bytes 786440 | tf_op jit(solution)/shard_map/ppermute | solution.py:644
  17.5 10.8 %collective-permute-start.2 = (bf16[128,1024]{1,0:T(8,128)(2,1)S(1)}, bf16[128,1024]{1,0:T(8,128)(2,1)S(1)}, u32[]{:S(2)}, u32[]{:S(2)}) collective-permute-start(bf16[128,1024]{1,0:T(8,128)(2,1)S(1)} %maximum_select_fusion.refs_0_), channel_id=1, source_target_pairs={{64,0},{72,8},{80,16},{88,24},{96,32},{104,40},{112,48},{120,56},{... | collective-permute-start | bytes 786440 | tf_op jit(solution)/shard_map/ppermute | solution.py:644
  17.5 14.2 %collective-permute-start.3 = (bf16[128,1024]{1,0:T(8,128)(2,1)S(1)}, bf16[128,1024]{1,0:T(8,128)(2,1)S(1)}, u32[]{:S(2)}, u32[]{:S(2)}) collective-permute-start(bf16[128,1024]{1,0:T(8,128)(2,1)S(1)} %maximum_select_fusion.refs_0_), channel_id=1, source_target_pairs={{96,0},{104,8},{112,16},{120,24},{0,32},{8,40},{16,48},{24,56},{32... | collective-permute-start | bytes 786440 | tf_op jit(solution)/shard_map/ppermute | solution.py:644
  28.2 3.4 %copy-start.7 = (bf16[128,1024]{1,0:T(8,128)(2,1)}, bf16[128,1024]{1,0:T(8,128)(2,1)S(1)}, u32[]{:S(2)}) copy-start(bf16[128,1024]{1,0:T(8,128)(2,1)S(1)} %collective-permute-done.1.refs_0_.refs_1_) | copy-start | bytes 786436
  28.3 3.4 %copy-start.8 = (bf16[128,1024]{1,0:T(8,128)(2,1)}, bf16[128,1024]{1,0:T(8,128)(2,1)S(1)}, u32[]{:S(2)}) copy-start(bf16[128,1024]{1,0:T(8,128)(2,1)S(1)} %collective-permute-done.2.refs_1_.refs_2_) | copy-start | bytes 786436
  31.7 0.7 copy-start.9
  32.4 18.2 %copy-start.3 = (s32[1024]{0:T(1024)S(1)}, s32[1024]{0:T(1024)}, u32[]{:S(2)}) copy-start(s32[1024]{0:T(1024)} %param.11) | copy-start | bytes 12292
  32.4 18.2 %copy-start.4 = (s32[32]{0:T(128)S(1)}, s32[32]{0:T(128)}, u32[]{:S(2)}) copy-start(s32[32]{0:T(128)} %param.12) | copy-start | bytes 388
  50.5 4.2 %collective-permute-start.5 = (bf16[32,128,256]{2,1,0:T(8,128)(2,1)S(1)}, bf16[32,128,256]{2,1,0:T(8,128)(2,1)S(1)}, u32[]{:S(2)}, u32[]{:S(2)}) collective-permute-start(bf16[32,128,256]{2,1,0:T(8,128)(2,1)S(1)} %bitcast.15), channel_id=1, source_target_pairs={{0,8},{8,0},{16,24},{24,16},{32,40},{40,32},{48,56},{56,48},{64,72... | collective-permute-start | bytes 6291464 | tf_op jit(solution)/shard_map/ppermute | solution.py:655
  63.6 3.8 %copy-start.2 = (s32[64]{0:T(128)S(1)}, s32[64]{0:T(128)}, u32[]{:S(2)}) copy-start(s32[64]{0:T(128)} %len_ref.1) | copy-start | bytes 772
  63.6 21.3 %all-to-all-start.1 = ((bf16[8,64,1152]{2,1,0:T(8,128)(2,1)}), bf16[8,64,1152]{2,1,0:T(8,128)(2,1)S(1)}, u32[]{:S(2)}, u32[]{:S(2)}) async-start(bf16[8,64,1152]{2,1,0:T(8,128)(2,1)} %bitcast.24), calls=%async_computation.1 | async-start | bytes 2359296 | tf_op jit(solution)/shard_map/all_to_all | solution.py:662
  84.8 25.5 %copy-start.1 = (bf16[512,640]{1,0:T(8,128)(2,1)S(1)}, bf16[512,640]{1,0:T(8,128)(2,1)}, u32[]{:S(2)}) copy-start(bf16[512,640]{1,0:T(8,128)(2,1)} %up_ref.1) | copy-start | bytes 1966084
